TPU v7x, 512 devices: a whole 4x4x16 slice. The times are simulated.
512 devices in a mesh: rows: 8 (over z_lo), chan: 64 (over y, x, z_hi, core).
Axes of the slice: x: 4, y: 4, z: 16 (z_hi: 2, z_lo: 8; z = z_hi * 8 + z_lo), core: 2. Of those that a mesh axis runs over, the one named last changes fastest.
Arguments:
- activations: bfloat16 [256, 7, 7, 512], P('rows', None, None, 'chan'), may hold values from 0 to 2
- cotangents: bfloat16 [256, 512, 49], P('rows', 'chan'), may hold values from -0.0005859375 to 0.0005859375
- ordering: int32 [8, 32], P('rows'), may hold values from 0 to 31, each once within a row
- ridge: float32 [128], replicated, may hold values from 0.2 to 2
Outputs:
- gram_panel: float32 [256, 128], P('rows')
- factor_panel: float32 [256, 128], P('rows')
Inputs may be any that keep to these rules, and one draw needn't show every extreme that they name: Each row of ordering lists every one of the group's 32 examples once.
All inputs are finite; a program needn't handle non-finite values.
Results may differ from a plain program's by a relative error of at most 0.0003.
Values may be sent and summed in bfloat16 or wider, within the bound.
A program may use at most 64 MiB of HBM per device.

v0:
```python
import jax
import jax.numpy as jnp
from jax import lax
from jax.sharding import PartitionSpec as P

PIV_DEV = 16


def jacobian_block(grad_rows, input_rows):
    example_count = input_rows.shape[0]
    side_len = input_rows.shape[1]
    channel_count = input_rows.shape[3]
    grad_count = grad_rows.shape[1]
    grid_grads = grad_rows.reshape(example_count, grad_count, side_len, side_len)
    padded_grads = jnp.pad(grid_grads, ((0, 0), (0, 0), (1, 1), (1, 1)))
    shifted = []
    for row_shift in range(3):
        for col_shift in range(3):
            window = padded_grads[
                :,
                :,
                2 - row_shift : 2 - row_shift + side_len,
                2 - col_shift : 2 - col_shift + side_len,
            ]
            shifted.append(window.reshape(example_count, grad_count, side_len * side_len))
    stacked_grads = jnp.stack(shifted, axis=2).reshape(
        example_count, grad_count * 9, side_len * side_len
    )
    flat_inputs = input_rows.reshape(example_count, side_len * side_len, channel_count)
    product = jnp.einsum(
        "nkp,npq->nkq", stacked_grads, flat_inputs, preferred_element_type=jnp.float32
    )
    return product.astype(jnp.bfloat16).reshape(example_count, -1)


def gram_block(left_rows, right_rows):
    return lax.dot_general(
        left_rows, right_rows, (((1,), (1,)), ((), ())), preferred_element_type=jnp.float32
    )


def local(activations, cotangents, ordering, ridge):
    local_order = ordering[0]
    own_inputs = jnp.take(activations, local_order, axis=0)
    own_grads = jnp.take(cotangents, local_order, axis=0)
    pivot_count = PIV_DEV
    pivot_inputs, pivot_grads = (
        lax.all_gather(own_inputs[:pivot_count], "rows", axis=0, tiled=True),
        lax.all_gather(own_grads[:pivot_count], "rows", axis=0, tiled=True),
    )
    full_own, full_pivot = (
        lax.all_gather(own_inputs, "chan", axis=3, tiled=True),
        lax.all_gather(pivot_inputs, "chan", axis=3, tiled=True),
    )
    own_jac = jacobian_block(own_grads, full_own)
    pivot_jac = jacobian_block(pivot_grads, full_pivot)
    partial_panel = gram_block(own_jac, pivot_jac)
    gram_panel = lax.psum(partial_panel, "chan")
    diag_block = lax.all_gather(gram_panel[:pivot_count], "rows", axis=0, tiled=True)
    system = 0.5 * (diag_block + diag_block.T) + jnp.diag(ridge)
    lower = jnp.linalg.cholesky(system)
    factor_panel = jax.scipy.linalg.solve_triangular(lower, gram_panel.T, lower=True).T
    return (gram_panel, factor_panel)


def solution(mesh):
    return jax.shard_map(
        local,
        mesh=mesh,
        in_specs=(P("rows", None, None, "chan"), P("rows", "chan", None), P("rows", None), P()),
        out_specs=(P("rows", None), P("rows", None)),
        check_vma=False,
    )
```

profile of v0, /device:TPU:1, one launch (start us, length us, event | category | flops | bytes accessed | tf_op | source)
XLA Modules:
  0.0 1025.0 jit_solution(938271558096505673)
XLA Ops:
  7.2 0.0 all-gather.3.cloned.1.call-start
  7.2 0.7 fusion.16
  7.9 0.7 compare_and_fusion
  8.6 1.2 copy.86
  9.8 0.6 gather_fusion.1
  10.4 0.1 broadcast_select_fusion
  10.5 0.9 copy.87
  11.5 0.0 all-gather.3.cloned.1.call-update
  11.5 0.0 all-gather.5.cloned.1.call-start
  11.6 55.5 %all_gather.17 = bf16[128,7,7,8]{3,2,1,0:T(8,128)(2,1)S(1)} all-gather(bf16[16,7,7,8]{3,2,1,0:T(8,128)(2,1)S(1)} %slice.96), channel_id=1, replica_groups=mesh['rows'=8,'chan'=64] {'rows'}, dimensions={0}, use_global_device_ids=true | all-gather | bytes 112896 | tf_op jit(solution)/shard_map/all_gather | solution.py:48
  67.0 2.7 copy.94
  69.8 0.0 all-gather.5.cloned.1.call-update
  69.8 0.6 gather_fusion
  70.4 0.2 copy.76
  70.6 0.1 slice_select_fusion
  70.7 43.9 %all_gather.16 = bf16[128,8,49]{2,1,0:T(8,128)(2,1)S(1)} all-gather(bf16[16,8,49]{2,1,0:T(8,128)(2,1)S(1)} %slice_select_fusion), channel_id=1, replica_groups=mesh['rows'=8,'chan'=64] {'rows'}, dimensions={0}, use_global_device_ids=true | all-gather | bytes 112896 | tf_op jit(solution)/shard_map/all_gather | solution.py:49
  114.6 0.2 copy.91
  114.8 0.1 pad_slice_fusion
  115.1 0.1 copy.93
  115.3 2.0 copy.96
  117.3 0.1 pad_slice_fusion.8
  117.4 0.2 copy.77
  117.6 0.2 copy.78
  117.8 0.2 copy.79
  117.9 0.2 copy.80
  118.1 0.2 copy.81
  118.3 0.2 copy.82
  118.4 0.2 copy.83
  118.6 0.2 copy.84
  118.8 0.1 fusion.15
  119.0 0.1 copy.85
  119.1 86.7 %all-gather.3.cloned.1.call-done = bf16[32,7,7,512]{0,3,2,1:T(8,128)(2,1)} async-done(((bf16[32,7,7,8]{0,3,2,1:T(8,128)(2,1)}), bf16[32,7,7,512]{0,3,2,1:T(8,128)(2,1)}) %all-gather.3.cloned.1.call-update) | async-done | bytes 1605648 | tf_op jit(solution)/shard_map/all_gather | solution.py:52
  205.8 7.6 copy.90
  213.4 3.8 convolution_convert_fusion.1
  217.1 161.6 %all-gather.5.cloned.1.call-done = bf16[128,7,7,512]{0,3,2,1:T(8,128)(2,1)} async-done(((bf16[128,7,7,8]{0,3,2,1:T(8,128)(2,1)}), bf16[128,7,7,512]{0,3,2,1:T(8,128)(2,1)}) %all-gather.5.cloned.1.call-update) | async-done | bytes 6422544 | tf_op jit(solution)/shard_map/all_gather | solution.py:53
  378.7 11.8 %copy.97 = bf16[128,49,512]{2,1,0:T(8,128)(2,1)} copy(bf16[128,49,512]{0,2,1:T(8,128)(2,1)} %bitcast.73) | data formatting | bytes 12845056 | tf_op jit(solution)/shard_map/reshape | solution.py:29
  390.5 5.9 convolution_convert_fusion
  396.4 9.4 fusion.3
  405.8 539.1 %psum.7 = f32[32,128]{1,0:T(8,128)S(1)} all-reduce(f32[32,128]{1,0:T(8,128)S(1)} %fusion.3), channel_id=1, replica_groups=mesh['rows'=8,'chan'=64] {'chan'}, use_global_device_ids=true, to_apply=%region_0.1 | all-reduce | flops 4096 | bytes 32768 | tf_op jit(solution)/shard_map/psum | solution.py:58
  944.9 49.3 %all_gather.19 = f32[128,128]{1,0:T(8,128)S(1)} all-gather(f32[16,128]{1,0:T(8,128)S(1)} %slice.97), channel_id=1, replica_groups=mesh['rows'=8,'chan'=64] {'rows'}, dimensions={0}, use_global_device_ids=true | all-gather | bytes 73728 | tf_op jit(solution)/shard_map/all_gather | solution.py:59
  994.2 0.1 copy.100
  994.3 0.1 fusion.14
  994.4 0.1 copy.101
  994.5 11.7 %cholesky.16 = f32[128,128]{1,0:T(8,128)S(1)} custom-call(f32[128,128]{1,0:T(8,128)S(1)} %fusion.12), custom_call_target="Cholesky" | custom-call | tf_op jit(solution)/shard_map/jit(cholesky)/cholesky | solution.py:61
  1006.3 0.6 compare_reduce_fusion
  1006.9 0.7 fusion.9
  1007.6 9.8 custom-call.7
  1017.4 0.8 fusion.10
  (29 shorter events, 0.4 us)
Async XLA Ops:
  7.2 62.6 %copy-start = (bf16[32,8,49]{2,1,0:T(8,128)(2,1)S(1)}, bf16[32,8,49]{2,1,0:T(8,128)(2,1)}, u32[]{:S(2)}) copy-start(bf16[32,8,49]{2,1,0:T(8,128)(2,1)} %param.5) | copy-start | bytes 75268
  7.2 198.6 %all-gather.3.cloned.1.call-start = ((), (), s32[]{:S(2)}) async-start(), calls=%async_computation | async-start | bytes 6522880 | tf_op jit(solution)/shard_map/all_gather | solution.py:52
  11.5 367.3 %all-gather.5.cloned.1.call-start = ((), (), s32[]{:S(2)}) async-start(), calls=%async_computation.1 | async-start | bytes 6522880 | tf_op jit(solution)/shard_map/all_gather | solution.py:53
  396.4 597.9 %copy-start.2 = (f32[128]{0:T(128)S(1)}, f32[128]{0:T(128)}, u32[]{:S(2)}) copy-start(f32[128]{0:T(128)} %param.7) | copy-start | bytes 1540
  944.9 73.3 %copy-start.1 = (f32[32,128]{1,0:T(8,128)}, f32[32,128]{1,0:T(8,128)S(1)}, u32[]{:S(2)}) copy-start(f32[32,128]{1,0:T(8,128)S(1)} %psum.7) | copy-start | bytes 49156
Sparse Core Ops, SparseCore 0:
  12.2 193.5 all-gather.2
  210.0 168.7 all-gather.4
where the time goes:
time: 1040 us; the launch traced here: 1020 us
  blocking collectives  688 us (66%)
  waiting for transfers between devices  248 us (24%)
  local copies, waits for them, and re-layouts  30 us (3%)
  other arithmetic  24.6 us (2%)
  matrix products  19.8 us (2%)
  between operations  14.3 us (1%)
    psum x1, blocking collectives, local(): gram_panel = lax.psum(partial_panel, 'chan')  539 us
    all_gather x1, waiting for transfers between devices, local(): lax.all_gather(pivot_inputs, 'chan', axis=3, tiled=True)  162 us
    all_gather x1, waiting for transfers between devices, local(): lax.all_gather(own_inputs, 'chan', axis=3, tiled=True)  86.7 us
    all_gather x1, blocking collectives, local(): lax.all_gather(own_inputs[:pivot_count], 'rows', axis=0, tiled=True)  55.5 us
    all_gather x1, blocking collectives, local(): lax.all_gather(gram_panel[:pivot_count], 'rows', axis=0, tiled=True)  49.3 us
    all_gather x1, blocking collectives, local(): lax.all_gather(own_grads[:pivot_count], 'rows', axis=0, tiled=True)  43.9 us
  transfers between devices with their start and end apart: 2, of which 2 were waited for; matrix products, arithmetic and copies ran while one was open for 2% of the time, Pallas kernels for 0%

commit v1 on v0

v1 whole, which is shorter than its diff:
```python
import functools

import jax
import jax.numpy as jnp
from jax import lax
from jax.experimental import pallas as pl
from jax.experimental.pallas import tpu as pltpu
from jax.sharding import PartitionSpec as P

F32 = jnp.float32
BF16 = jnp.bfloat16
MESH = pl.DeviceIdType.MESH
VM = pl.BlockSpec(memory_space=pltpu.VMEM)
SM = pl.BlockSpec(memory_space=pltpu.SMEM)


def place():
    k = lax.axis_index("rows")
    j = lax.axis_index("chan")
    return k, j // 4, (j // 2) % 2, j % 2


def dev(k, yx, zh, c):
    return {"rows": k, "chan": (yx * 2 + zh) * 2 + c}


def plane_peer(a, i):
    other = (a + i) % 32
    return other // 2, other % 2


def z_dev(z, yx, c):
    z = z % 16
    return dev(z % 8, yx, z // 8, c)


def prep_kernel(order_ref, x_ref, g_ref, out_ref, ge, go, xs):
    _, _, _, c = place()
    pos = lax.broadcasted_iota(jnp.int32, (49, 128), 0)
    lane = lax.broadcasted_iota(jnp.int32, (49, 128), 1)
    slot = (pos // 7) * 8 + pos % 7
    low = jnp.where(lane == slot, 1.0, 0.0).astype(BF16)
    high = jnp.where(lane == slot + 64, 1.0, 0.0).astype(BF16)
    for u in range(16):
        ge[pl.ds(u * 8, 8), :] = g_ref[order_ref[0, 2 * u]].astype(F32)
        go[pl.ds(u * 8, 8), :] = g_ref[order_ref[0, 2 * u + 1]].astype(F32)
    grads = jnp.dot(ge[...].astype(BF16), low, preferred_element_type=F32) + jnp.dot(
        go[...].astype(BF16), high, preferred_element_type=F32
    )
    grads = grads.reshape(16, 8, 128)
    unit = lax.broadcasted_iota(jnp.int32, (16, 32), 0)
    example = lax.broadcasted_iota(jnp.int32, (16, 32), 1)
    even = jnp.zeros((16, 32), F32)
    odd = jnp.zeros((16, 32), F32)
    for u in range(16):
        even = jnp.where((unit == u) & (example == order_ref[0, 2 * u]), 1.0, even)
        odd = jnp.where((unit == u) & (example == order_ref[0, 2 * u + 1]), 1.0, odd)
    even = even.astype(BF16)
    odd = odd.astype(BF16)
    for ch in range(8):
        block = x_ref[:, ch, :]
        dims = (((0,), (0,)), ((), ()))
        at_low = lax.dot_general(block, low, dims, preferred_element_type=F32).astype(BF16)
        at_high = lax.dot_general(block, high, dims, preferred_element_type=F32).astype(BF16)
        xs[:, ch, :] = jnp.dot(even, at_low, preferred_element_type=F32) + jnp.dot(
            odd, at_high, preferred_element_type=F32
        )
    inputs = xs[...]
    first = jnp.where(c == 0, grads, inputs)
    second = jnp.where(c == 0, inputs, grads)
    out_ref[...] = jnp.concatenate([first, second], axis=1).astype(BF16)


def prep(order, x, g):
    return pl.pallas_call(
        prep_kernel,
        out_shape=jax.ShapeDtypeStruct((16, 16, 128), BF16),
        in_specs=[SM, VM, VM],
        out_specs=VM,
        scratch_shapes=[
            pltpu.VMEM((128, 49), F32),
            pltpu.VMEM((128, 49), F32),
            pltpu.VMEM((16, 8, 128), F32),
        ],
        name="prep",
    )(order, x, g)


def gather_kernel(t_ref, rows_ref, piv_ref, mate_ref, mate_sem, row_send, row_recv, a2a_send, a2a_recv,
                  ring_send, ring_recv, sib_send, sib_recv):
    k, yx, zh, c = place()
    z = zh * 8 + k
    a = yx * 2 + c
    par = yx % 2
    away = (k + par) % 2
    slot_of = (zh * 2 + c) * 16 + yx
    mate_slot = ((1 - zh) * 2 + c) * 16 + yx
    mate_dev = dev(k, yx, 1 - zh, c)
    sib_dev = dev(k, yx, zh, 1 - c)

    barrier = pltpu.get_barrier_semaphore()

    @pl.loop(1, 32)
    def _(i):
        yx2, c2 = plane_peer(a, i)
        pl.semaphore_signal(barrier, inc=1, device_id=dev(k, yx2, zh, c2), device_id_type=MESH)

    for other in (mate_dev, z_dev(z + 1, yx, c), z_dev(z + 15, yx, c)):
        pl.semaphore_signal(barrier, inc=1, device_id=other, device_id_type=MESH)
    pl.semaphore_wait(barrier, 34)

    to_mate = pltpu.make_async_remote_copy(
        src_ref=t_ref.at[pl.ds(8 * (1 - zh), 8)], dst_ref=mate_ref,
        send_sem=mate_sem.at[0], recv_sem=mate_sem.at[1], device_id=mate_dev, device_id_type=MESH)
    to_mate.start()

    own_chunk = ((k // 2) * 2 + zh) * 2 + c
    for u in range(8):
        target = (u // 2) * 4 + 2 * (u % 2) + k % 2

        @pl.when(target == yx)
        def _():
            pltpu.make_async_copy(t_ref.at[u], piv_ref.at[own_chunk, yx], a2a_recv.at[0]).start()

        @pl.when(target != yx)
        def _():
            pltpu.make_async_remote_copy(
                src_ref=t_ref.at[u], dst_ref=piv_ref.at[own_chunk, yx],
                send_sem=a2a_send.at[0], recv_sem=a2a_recv.at[0],
                device_id=dev(k, target, zh, c), device_id_type=MESH).start()

    def send_rows(src_ref, base, slot):
        @pl.loop(1, 32)
        def _(i):
            yx2, c2 = plane_peer(a, i)
            pltpu.make_async_remote_copy(
                src_ref=src_ref.at[pl.ds(base + 4 * c2, 4)], dst_ref=rows_ref.at[slot],
                send_sem=row_send.at[0], recv_sem=row_recv.at[0],
                device_id=dev(k, yx2, zh, c2), device_id_type=MESH).start()

        pltpu.make_async_copy(src_ref.at[pl.ds(base + 4 * c, 4)], rows_ref.at[slot], row_recv.at[0]).start()

    def ring_copy(chunk, right, slot_send, slot_recv):
        way = 0 if right else 1
        target = z_dev(z + 1, yx, c) if right else z_dev(z + 15, yx, c)
        return pltpu.make_async_remote_copy(
            src_ref=piv_ref.at[chunk], dst_ref=piv_ref.at[chunk],
            send_sem=ring_send.at[way, slot_send], recv_sem=ring_recv.at[way, slot_recv],
            device_id=target, device_id_type=MESH)

    def sib_copy(chunk):
        return pltpu.make_async_remote_copy(
            src_ref=piv_ref.at[chunk], dst_ref=piv_ref.at[chunk],
            send_sem=sib_send.at[0], recv_sem=sib_recv.at[0],
            device_id=sib_dev, device_id_type=MESH)

    send_rows(t_ref, 8 * zh, slot_of)

    @pl.when(away == 0)
    def _():
        pltpu.make_async_copy(piv_ref.at[own_chunk], piv_ref.at[own_chunk], a2a_recv.at[0]).wait()
        ring_copy(own_chunk, True, 4, 0).start()
        ring_copy(own_chunk, False, 4, 0).start()
        sib_copy(own_chunk).start()

    to_mate.wait_recv()
    send_rows(mate_ref, 0, mate_slot)

    for n in range(4):
        dist = 2 * n + 2 - away
        for right in (True, False):
            src_z = (z + 16 - dist) % 16 if right else (z + dist) % 16
            chunk = (((src_z % 8) // 2) * 2 + src_z // 8) * 2 + c

            def arrive(right=right, chunk=chunk, n=n):
                ring_copy(chunk, right, n, n).wait_recv()

            def forward(right=right, chunk=chunk, n=n):
                ring_copy(chunk, right, n, n + 1 - away).start()

            if n < 3:
                arrive()
                forward()
                sib_copy(chunk).start()
            elif right:
                arrive()

                @pl.when(away == 1)
                def _():
                    forward()

                sib_copy(chunk).start()
            else:

                @pl.when(away == 1)
                def _():
                    arrive()
                    sib_copy(chunk).start()

    to_mate.wait_send()

    @pl.when(away == 0)
    def _():
        pltpu.make_async_copy(t_ref.at[pl.ds(0, 7)], t_ref.at[pl.ds(0, 7)], a2a_send.at[0]).wait()
        for right in (True, False):
            ring_copy(own_chunk, right, 4, 0).wait_send()
            for n in range(3):
                ring_copy(own_chunk, right, n, 0).wait_send()

    @pl.when(away == 1)
    def _():
        pltpu.make_async_copy(t_ref.at[pl.ds(0, 8)], t_ref.at[pl.ds(0, 8)], a2a_send.at[0]).wait()
        for n in range(4):
            ring_copy(own_chunk, True, n, 0).wait_send()
        for n in range(3):
            ring_copy(own_chunk, False, n, 0).wait_send()

    pltpu.make_async_copy(rows_ref.at[pl.ds(0, 62)], rows_ref.at[pl.ds(0, 62)], row_send.at[0]).wait()
    pltpu.make_async_copy(rows_ref, rows_ref, row_recv.at[0]).wait()
    pltpu.make_async_copy(piv_ref.at[pl.ds(0, 8)], piv_ref.at[pl.ds(0, 8)], sib_send.at[0]).wait()
    pltpu.make_async_copy(piv_ref.at[pl.ds(0, 8)], piv_ref.at[pl.ds(0, 8)], sib_recv.at[0]).wait()


def gather(t):
    return pl.pallas_call(
        gather_kernel,
        out_shape=[
            jax.ShapeDtypeStruct((64, 4, 16, 128), BF16),
            jax.ShapeDtypeStruct((16, 16, 16, 128), BF16),
        ],
        in_specs=[VM],
        out_specs=[VM, VM],
        scratch_shapes=[
            pltpu.VMEM((8, 16, 128), BF16),
            pltpu.SemaphoreType.DMA((2,)),
            pltpu.SemaphoreType.DMA((1,)),
            pltpu.SemaphoreType.DMA((1,)),
            pltpu.SemaphoreType.DMA((1,)),
            pltpu.SemaphoreType.DMA((1,)),
            pltpu.SemaphoreType.DMA((2, 5)),
            pltpu.SemaphoreType.DMA((2, 4)),
            pltpu.SemaphoreType.DMA((1,)),
            pltpu.SemaphoreType.DMA((1,)),
        ],
        compiler_params=pltpu.CompilerParams(
            collective_id=0, has_side_effects=True, vmem_limit_bytes=16 * 1024 * 1024),
        name="gather_inputs",
    )(t)


def block_kernel(rows_ref, piv_ref, out_ref, ag, ax, bg, bx, gg, xx):
    k, yx, zh, c = place()
    mask = lax.broadcasted_iota(jnp.int32, (16, 16, 128), 1) < 8

    for z2 in range(2):
        for u in range(4):
            even = rows_ref[pl.ds(z2 * 32, 16), u]
            odd = rows_ref[pl.ds(z2 * 32 + 16, 16), u]
            ag[pl.ds(z2 * 256, 256), pl.ds(u * 128, 128)] = jnp.where(mask, even, odd).reshape(256, 128)
            ax[pl.ds(z2 * 256, 256), pl.ds(u * 128, 128)] = jnp.where(mask, odd, even).reshape(256, 128)
            even = piv_ref[(u * 2 + z2) * 2]
            odd = piv_ref[(u * 2 + z2) * 2 + 1]
            bg[pl.ds(z2 * 256, 256), pl.ds(u * 128, 128)] = jnp.where(mask, even, odd).reshape(256, 128)
            bx[pl.ds(z2 * 256, 256), pl.ds(u * 128, 128)] = jnp.where(mask, odd, even).reshape(256, 128)
    dims = (((0,), (0,)), ((), ()))
    gg[...] = lax.dot_general(ag[...], bg[...], dims, preferred_element_type=F32)
    xx[...] = lax.dot_general(ax[...], bx[...], dims, preferred_element_type=F32)
    lanes = lax.broadcasted_iota(jnp.int32, (128, 128), 0)
    cols = lax.broadcasted_iota(jnp.int32, (128, 128), 1)
    piv0 = 16 * (yx % 2) + 2 * ((yx // 4) * 2 + (yx % 4) // 2)
    pieces = jnp.zeros((8, 128), F32)
    for t in range(4):
        col = pl.ds(t * 128, 128)
        summed = []
        for e in range(8):
            wide = xx[pl.ds(e * 64, 64), col]
            wide = (
                wide
                + pltpu.roll(pltpu.roll(wide, 1, 0), 1, 1)
                + pltpu.roll(pltpu.roll(wide, 63, 0), 127, 1)
            )
            wide = (
                wide
                + pltpu.roll(pltpu.roll(wide, 8, 0), 8, 1)
                + pltpu.roll(pltpu.roll(wide, 56, 0), 120, 1)
            )
            summed.append(jnp.sum(gg[pl.ds(e * 64, 64), col] * wide, axis=0, keepdims=True))
        folded = jnp.concatenate(summed, axis=0)
        spread = jnp.where(cols == piv0 + 32 * t + lanes // 64, 1.0, 0.0)
        pieces = pieces + jnp.dot(folded, spread, precision=lax.Precision.HIGHEST, preferred_element_type=F32)
    out_ref[...] = pieces


def block(rows, piv):
    return pl.pallas_call(
        block_kernel,
        out_shape=jax.ShapeDtypeStruct((8, 128), F32),
        in_specs=[VM, VM],
        out_specs=VM,
        scratch_shapes=[pltpu.VMEM((512, 512), BF16)] * 4 + [pltpu.VMEM((512, 512), F32)] * 2,
        compiler_params=pltpu.CompilerParams(vmem_limit_bytes=24 * 1024 * 1024),
        name="kernel_block",
    )(rows, piv)


def panel_kernel(part_ref, diag_ref, rest_ref, parts, plane_rows, send1, recv1, send2, recv2, recv3):
    k, yx, zh, c = place()
    z = zh * 8 + k
    a = yx * 2 + c
    barrier = pltpu.get_barrier_semaphore()

    @pl.loop(1, 32)
    def _(i):
        yx2, c2 = plane_peer(a, i)
        pl.semaphore_signal(barrier, inc=1, device_id=dev(k, yx2, zh, c2), device_id_type=MESH)

    @pl.loop(1, 16)
    def _(i):
        pl.semaphore_signal(barrier, inc=1, device_id=z_dev(z + i, yx, c), device_id_type=MESH)

    pl.semaphore_wait(barrier, 46)

    slot = c * 16 + yx

    @pl.loop(1, 32)
    def _(i):
        yx2, c2 = plane_peer(a, i)
        pltpu.make_async_remote_copy(
            src_ref=part_ref, dst_ref=parts.at[slot], send_sem=send1.at[0], recv_sem=recv1.at[0],
            device_id=dev(k, yx2, zh, c2), device_id_type=MESH).start()

    pltpu.make_async_copy(part_ref, parts.at[slot], recv1.at[0]).start()
    pltpu.make_async_copy(parts, parts, recv1.at[0]).wait()
    for c2 in range(2):
        plane_rows[pl.ds(c2 * 8, 8), :] = jnp.sum(parts[pl.ds(c2 * 16, 16)], axis=0)

    @pl.when(zh == 0)
    def _():
        @pl.loop(1, 16)
        def _(i):
            pltpu.make_async_remote_copy(
                src_ref=plane_rows, dst_ref=diag_ref.at[k], send_sem=send2.at[0], recv_sem=recv2.at[0],
                device_id=z_dev(z + i, yx, c), device_id_type=MESH).start()

        pltpu.make_async_copy(plane_rows, diag_ref.at[k], recv2.at[0]).start()

    @pl.when(zh == 1)
    def _():
        pltpu.make_async_remote_copy(
            src_ref=plane_rows, dst_ref=rest_ref, send_sem=send2.at[0], recv_sem=recv3.at[0],
            device_id=dev(k, yx, 0, c), device_id_type=MESH).start()
        pltpu.make_async_copy(plane_rows, rest_ref, recv3.at[0]).start()

    pltpu.make_async_copy(diag_ref, diag_ref, recv2.at[0]).wait()
    pltpu.make_async_copy(rest_ref, rest_ref, recv3.at[0]).wait()
    pltpu.make_async_copy(parts.at[pl.ds(0, 31)], parts.at[pl.ds(0, 31)], send1.at[0]).wait()

    @pl.when(zh == 0)
    def _():
        pltpu.make_async_copy(parts.at[pl.ds(0, 30)], parts.at[pl.ds(0, 30)], send2.at[0]).wait()

    @pl.when(zh == 1)
    def _():
        pltpu.make_async_copy(plane_rows, plane_rows, send2.at[0]).wait()


def panel(part):
    return pl.pallas_call(
        panel_kernel,
        out_shape=[jax.ShapeDtypeStruct((8, 16, 128), F32), jax.ShapeDtypeStruct((16, 128), F32)],
        in_specs=[VM],
        out_specs=[VM, VM],
        scratch_shapes=[
            pltpu.VMEM((32, 8, 128), F32),
            pltpu.VMEM((16, 128), F32),
        ] + [pltpu.SemaphoreType.DMA((1,))] * 5,
        compiler_params=pltpu.CompilerParams(collective_id=1, has_side_effects=True),
        name="gather_panel",
    )(part)


def solve_kernel(diag_ref, rest_ref, ridge_ref, gram_ref, factor_ref):
    k, _, _, _ = place()
    gram_ref[pl.ds(0, 16), :] = diag_ref[k]
    gram_ref[pl.ds(16, 16), :] = rest_ref[...]
    gram = gram_ref[...]
    diag = diag_ref[...].reshape(128, 128)
    row = lax.broadcasted_iota(jnp.int32, (128, 128), 0)
    col = lax.broadcasted_iota(jnp.int32, (128, 128), 1)
    system = 0.5 * (diag + diag.T) + jnp.where(row == col, ridge_ref[...], 0.0)
    right = jnp.concatenate([gram, jnp.zeros((96, 128), F32)], axis=0).T
    sub = lax.broadcasted_iota(jnp.int32, (8, 128), 0)
    left = [system[8 * m:8 * m + 8] for m in range(16)]
    right = [right[8 * m:8 * m + 8] for m in range(16)]
    for j in range(128):
        m0, i = j // 8, j % 8
        pivot_row = left[m0][i:i + 1, :]
        right_row = right[m0][i:i + 1, :]
        pivot = left[m0][i:i + 1, j:j + 1]
        inverse = 1.0 / pivot
        scaled_row = pivot_row * inverse
        scaled_right = right_row * inverse
        for m in range(m0, 16):
            factor = jnp.broadcast_to(left[m][:, j:j + 1], (8, 128))
            if m == m0:
                factor = jnp.where(sub > i, factor, 0.0)
            left[m] = left[m] - factor * scaled_row
            right[m] = right[m] - factor * scaled_right
    lane = lax.broadcasted_iota(jnp.int32, (8, 128), 1)
    for m in range(16):
        pivots = jnp.sum(jnp.where(lane == sub + 8 * m, left[m], 0.0), axis=1, keepdims=True)
        right[m] = right[m] * lax.rsqrt(pivots)
    factor_ref[...] = jnp.concatenate(right, axis=0).T[:32]


def solve(diag, rest, ridge):
    out = jax.ShapeDtypeStruct((32, 128), F32)
    return pl.pallas_call(
        solve_kernel,
        out_shape=[out, out],
        in_specs=[VM, VM, VM],
        out_specs=[VM, VM],
        name="factor_solve",
    )(diag, rest, ridge)


def local(activations, cotangents, ordering, ridge):
    x = activations.transpose(1, 2, 3, 0).reshape(49, 8, 32)
    t = prep(ordering, x, cotangents)
    rows, piv = gather(t)
    part = block(rows, piv)
    diag, rest = panel(part)
    return tuple(solve(diag, rest, ridge.reshape(1, 128)))


def solution(mesh):
    return jax.shard_map(
        local,
        mesh=mesh,
        in_specs=(P("rows", None, None, "chan"), P("rows", "chan", None), P("rows", None), P()),
        out_specs=(P("rows", None), P("rows", None)),
        check_vma=False,
    )
```

time: 1040 us -> 95.5 us (0.09); the launches traced: 1020 us -> 95.2 us
  blocking collectives: 688 us -> 0 us
  waiting for transfers between devices: 248 us -> 0 us
  Pallas kernels: 0 us -> 93.1 us
  local copies, waits for them, and re-layouts: 30 us -> 1.44 us
  other arithmetic: 24.6 us -> 0 us
  matrix products: 19.8 us -> 0 us
  between operations: 14.3 us -> 0.65 us
    psum x1 -> x0, blocking collectives: 539 us -> none  [local(): gram_panel = lax.psum(partial_panel, 'chan')]
    all_gather x2 -> x0, waiting for transfers between devices: 248 us -> none  [the longest x1 162 us: local(): lax.all_gather(pivot_inputs, 'chan', axis=3, tiled=True)]
    all_gather x3 -> x0, blocking collectives: 149 us -> none  [the longest x1 55.5 us: local(): lax.all_gather(own_inputs[:pivot_count], 'rows', axis=0, tiled=True)]
    pallas_call x0 -> x5, Pallas kernels: none -> 93.1 us  [the longest x1 49.8 us: gather(): pl.pallas_call(gather_kernel, out_shape=[jax.ShapeDtypeStruct((64, 4, 16,...]
    another operation x5 -> x0, other arithmetic: 22.9 us -> none  [the longest x3 12.4 us: local(): lower = jnp.linalg.cholesky(system)]
    reshape x3 -> x0, local copies, waits for them, and re-layouts: 21.4 us -> none  [the longest x2 19.4 us: jacobian_block(): input_rows.reshape(example_count, side_len * side_len, channel_count)]
    dot_general x3 -> x0, matrix products: 19.1 us -> none  [the longest x2 9.62 us: jacobian_block(): jnp.einsum('nkp,npq->nkq', stacked_grads, flat_inputs, preferred_element_...]
  transfers between devices with their start and end apart: 2 -> 0, of which waited for: 2 -> 0; matrix products, arithmetic and copies ran while one was open for 2% -> 0% of each run, Pallas kernels for 0% -> 0%
where the time goes in v1:
time: 95.5 us; the launch traced here: 95.2 us
  Pallas kernels  93.1 us (97%)
  local copies, waits for them, and re-layouts  1.44 us (2%)
    pallas_call x1, Pallas kernels, gather(): pl.pallas_call(gather_kernel, out_shape=[jax.ShapeDtypeStruct((64, 4, 16,...  49.8 us
    pallas_call x1, Pallas kernels, panel(): pl.pallas_call(panel_kernel, out_shape=[jax.ShapeDtypeStruct((8, 16, 128)...  25.2 us
    pallas_call x1, Pallas kernels, solve(): pl.pallas_call(solve_kernel, out_shape=[out, out], in_specs=[VM, VM, VM],...  12.5 us
    pallas_call x1, Pallas kernels, block(): pl.pallas_call(block_kernel, out_shape=jax.ShapeDtypeStruct((8, 128), F32...  2.85 us
    pallas_call x1, Pallas kernels, prep(): pl.pallas_call(prep_kernel, out_shape=jax.ShapeDtypeStruct((16, 16, 128),...  2.82 us

profile of v1, /device:TPU:1, one launch (start us, length us, event | category | flops | bytes accessed | tf_op | source)
XLA Modules:
  0.0 95.2 jit_solution(16758101010899342905)
XLA Ops:
  0.6 2.8 %prep.1.t_ref = bf16[16,16,128]{2,1,0:T(8,128)(2,1)} custom-call(s32[1,32]{1,0:T(1,128)} %order_ref.1, bf16[49,8,32]{2,1,0:T(8,128)(2,1)} %bitcast.4, bf16[32,8,49]{2,1,0:T(8,128)(2,1)} %g_ref.1), custom_call_target="tpu_custom_call" | custom-call | tf_op jit(solution)/shard_map/prep/pallas_call | solution.py:75
  3.4 0.0 copy-start
  3.5 0.8 copy-done
  4.3 49.8 %gather_inputs.1 = (bf16[64,4,16,128]{3,2,1,0:T(8,128)(2,1)S(1)}, bf16[16,16,16,128]{3,2,1,0:T(8,128)(2,1)S(1)}) custom-call(bf16[16,16,128]{2,1,0:T(8,128)(2,1)S(1)} %copy-done), custom_call_target="tpu_custom_call" | custom-call | tf_op jit(solution)/shard_map/gather_inputs/pallas_call | solution.py:225
  54.1 2.9 %kernel_block.1.part_ref = f32[8,128]{1,0:T(8,128)S(1)} custom-call(bf16[64,4,16,128]{3,2,1,0:T(8,128)(2,1)S(1)} %get-tuple-element.6.rows_ref, bf16[16,16,16,128]{3,2,1,0:T(8,128)(2,1)S(1)} %get-tuple-element.7.piv_ref), custom_call_target="tpu_custom_call" | custom-call | tf_op jit(solution)/shard_map/kernel_block/pallas_call | solution.py:295
  57.0 0.0 copy-start.1
  57.0 0.6 copy-done.1
  57.6 25.2 %gather_panel.1 = (f32[8,16,128]{2,1,0:T(8,128)}, f32[16,128]{1,0:T(8,128)}) custom-call(f32[8,128]{1,0:T(8,128)} %copy-done.1), custom_call_target="tpu_custom_call" | custom-call | tf_op jit(solution)/shard_map/gather_panel/pallas_call | solution.py:368
  82.8 12.5 %factor_solve.1 = (f32[32,128]{1,0:T(8,128)}, f32[32,128]{1,0:T(8,128)}) custom-call(f32[8,16,128]{2,1,0:T(8,128)} %get-tuple-element.8.diag_ref, f32[16,128]{1,0:T(8,128)} %get-tuple-element.9.rest_ref, f32[1,128]{1,0:T(1,128)} %bitcast.5), custom_call_target="tpu_custom_call" | custom-call | tf_op jit(solution)/shard_map/factor_solve/pallas_call | solution.py:418
Async XLA Ops:
  3.4 0.8 copy-start
  57.0 0.6 copy-start.1

commit v2 on v1

v2 whole, which is shorter than its diff:
```python
import functools

import jax
import jax.numpy as jnp
from jax import lax
from jax.experimental import pallas as pl
from jax.experimental.pallas import tpu as pltpu
from jax.sharding import PartitionSpec as P

F32 = jnp.float32
BF16 = jnp.bfloat16
MESH = pl.DeviceIdType.MESH
VM = pl.BlockSpec(memory_space=pltpu.VMEM)
SM = pl.BlockSpec(memory_space=pltpu.SMEM)


def place():
    k = lax.axis_index("rows")
    j = lax.axis_index("chan")
    return k, j // 4, (j // 2) % 2, j % 2


def dev(k, yx, zh, c):
    return {"rows": k, "chan": (yx * 2 + zh) * 2 + c}


def plane_peer(a, i):
    other = (a + i) % 32
    return other // 2, other % 2


def z_dev(z, yx, c):
    z = z % 16
    return dev(z % 8, yx, z // 8, c)


def lay_out(order_ref, x_ref, g_ref, out_ref, ge, go, xs, c):
    pos = lax.broadcasted_iota(jnp.int32, (49, 128), 0)
    lane = lax.broadcasted_iota(jnp.int32, (49, 128), 1)
    slot = (pos // 7) * 8 + pos % 7
    low = jnp.where(lane == slot, 1.0, 0.0).astype(BF16)
    high = jnp.where(lane == slot + 64, 1.0, 0.0).astype(BF16)
    for u in range(16):
        ge[pl.ds(u * 8, 8), :] = g_ref[order_ref[0, 2 * u]].astype(F32)
        go[pl.ds(u * 8, 8), :] = g_ref[order_ref[0, 2 * u + 1]].astype(F32)
    grads = jnp.dot(ge[...].astype(BF16), low, preferred_element_type=F32) + jnp.dot(
        go[...].astype(BF16), high, preferred_element_type=F32
    )
    grads = grads.reshape(16, 8, 128)
    unit = lax.broadcasted_iota(jnp.int32, (16, 32), 0)
    example = lax.broadcasted_iota(jnp.int32, (16, 32), 1)
    even = jnp.zeros((16, 32), F32)
    odd = jnp.zeros((16, 32), F32)
    for u in range(16):
        even = jnp.where((unit == u) & (example == order_ref[0, 2 * u]), 1.0, even)
        odd = jnp.where((unit == u) & (example == order_ref[0, 2 * u + 1]), 1.0, odd)
    even = even.astype(BF16)
    odd = odd.astype(BF16)
    for ch in range(8):
        part = x_ref[:, ch, :]
        dims = (((0,), (0,)), ((), ()))
        at_low = lax.dot_general(part, low, dims, preferred_element_type=F32).astype(BF16)
        at_high = lax.dot_general(part, high, dims, preferred_element_type=F32).astype(BF16)
        xs[:, ch, :] = jnp.dot(even, at_low, preferred_element_type=F32) + jnp.dot(
            odd, at_high, preferred_element_type=F32
        )
    inputs = xs[...]
    first = jnp.where(c == 0, grads, inputs)
    second = jnp.where(c == 0, inputs, grads)
    out_ref[...] = jnp.concatenate([first, second], axis=1).astype(BF16)


def block(rows_ref, piv_ref, out_ref, ag, ax, bg, bx, gg, xx, yx):
    mask = lax.broadcasted_iota(jnp.int32, (16, 16, 128), 1) < 8
    for z2 in range(2):
        for u in range(4):
            even = rows_ref[pl.ds(z2 * 32, 16), u]
            odd = rows_ref[pl.ds(z2 * 32 + 16, 16), u]
            ag[pl.ds(z2 * 256, 256), pl.ds(u * 128, 128)] = jnp.where(mask, even, odd).reshape(256, 128)
            ax[pl.ds(z2 * 256, 256), pl.ds(u * 128, 128)] = jnp.where(mask, odd, even).reshape(256, 128)
            even = piv_ref[(u * 2 + z2) * 2]
            odd = piv_ref[(u * 2 + z2) * 2 + 1]
            bg[pl.ds(z2 * 256, 256), pl.ds(u * 128, 128)] = jnp.where(mask, even, odd).reshape(256, 128)
            bx[pl.ds(z2 * 256, 256), pl.ds(u * 128, 128)] = jnp.where(mask, odd, even).reshape(256, 128)
    dims = (((0,), (0,)), ((), ()))
    gg[...] = lax.dot_general(ag[...], bg[...], dims, preferred_element_type=F32)
    xx[...] = lax.dot_general(ax[...], bx[...], dims, preferred_element_type=F32)
    lanes = lax.broadcasted_iota(jnp.int32, (128, 128), 0)
    cols = lax.broadcasted_iota(jnp.int32, (128, 128), 1)
    piv0 = 16 * (yx % 2) + 2 * ((yx // 4) * 2 + (yx % 4) // 2)
    pieces = jnp.zeros((8, 128), F32)
    for t in range(4):
        col = pl.ds(t * 128, 128)
        summed = []
        for e in range(8):
            wide = xx[pl.ds(e * 64, 64), col]
            wide = (
                wide
                + pltpu.roll(pltpu.roll(wide, 1, 0), 1, 1)
                + pltpu.roll(pltpu.roll(wide, 63, 0), 127, 1)
            )
            wide = (
                wide
                + pltpu.roll(pltpu.roll(wide, 8, 0), 8, 1)
                + pltpu.roll(pltpu.roll(wide, 56, 0), 120, 1)
            )
            summed.append(jnp.sum(gg[pl.ds(e * 64, 64), col] * wide, axis=0, keepdims=True))
        folded = jnp.concatenate(summed, axis=0)
        spread = jnp.where(cols == piv0 + 32 * t + lanes // 64, 1.0, 0.0)
        pieces = pieces + jnp.dot(folded, spread, precision=lax.Precision.HIGHEST, preferred_element_type=F32)
    out_ref[...] = pieces


def panel_kernel(order_ref, x_ref, g_ref, diag_ref, rest_ref,
                 ge, go, xs, t_ref, mate_ref, rows_ref, piv_ref, ag, ax, bg, bx, gg, xx, part_ref, parts, plane_rows,
                 mate_sem, row_send, row_recv, a2a_send, a2a_recv, hub_send, hub_recv, near_send, near_recv,
                 sib_send, sib_recv, send1, recv1, send2, recv2, recv3):
    k, yx, zh, c = place()
    z = zh * 8 + k
    a = yx * 2 + c
    away = (k + yx) % 2
    mate_dev = dev(k, yx, 1 - zh, c)
    sib_dev = dev(k, yx, zh, 1 - c)

    barrier = pltpu.get_barrier_semaphore()

    @pl.loop(1, 32)
    def _(i):
        yx2, c2 = plane_peer(a, i)
        pl.semaphore_signal(barrier, inc=1, device_id=dev(k, yx2, zh, c2), device_id_type=MESH)

    @pl.loop(1, 16)
    def _(i):
        pl.semaphore_signal(barrier, inc=1, device_id=z_dev(z + i, yx, c), device_id_type=MESH)

    lay_out(order_ref, x_ref, g_ref, t_ref, ge, go, xs, c)
    pl.semaphore_wait(barrier, 46)

    def remote(src, dst, send, recv, target):
        return pltpu.make_async_remote_copy(
            src_ref=src, dst_ref=dst, send_sem=send, recv_sem=recv, device_id=target, device_id_type=MESH)

    def drain(ref, sem):
        pltpu.make_async_copy(ref, ref, sem).wait()

    to_mate = remote(t_ref.at[pl.ds(8 * (1 - zh), 8)], mate_ref, mate_sem.at[0], mate_sem.at[1], mate_dev)
    to_mate.start()

    def chunk_of(src_z):
        src_z = (src_z + 32) % 16
        return (((src_z % 8) // 2) * 2 + src_z // 8) * 2 + c

    own_chunk = chunk_of(z)
    for u in range(8):
        target = (u // 2) * 4 + 2 * (u % 2) + k % 2

        @pl.when(target == yx)
        def _():
            pltpu.make_async_copy(t_ref.at[u], piv_ref.at[own_chunk, yx], a2a_recv.at[0]).start()

        @pl.when(target != yx)
        def _():
            remote(t_ref.at[u], piv_ref.at[own_chunk, yx], a2a_send.at[0], a2a_recv.at[0],
                   dev(k, target, zh, c)).start()

    def send_rows(src_ref, base, slot):
        @pl.loop(1, 32)
        def _(i):
            yx2, c2 = plane_peer(a, i)
            remote(src_ref.at[pl.ds(base + 4 * c2, 4)], rows_ref.at[slot], row_send.at[0], row_recv.at[0],
                   dev(k, yx2, zh, c2)).start()

        pltpu.make_async_copy(src_ref.at[pl.ds(base + 4 * c, 4)], rows_ref.at[slot], row_recv.at[0]).start()

    def piv_copy(chunk, target, send, recv):
        return remote(piv_ref.at[chunk], piv_ref.at[chunk], send, recv, target)

    def sib_copy(chunk):
        return piv_copy(chunk, sib_dev, sib_send.at[0], sib_recv.at[0])

    hub = (0, -4, 4, 8)

    def near(role, step, n, recv):
        return piv_copy(chunk_of(z + hub[role]), z_dev(z + 16 + step, yx, c), near_send.at[n], near_recv.at[recv])

    nears = [(0, 1, 0), (0, -1, 4), (0, 2, 0), (0, -2, 2),
             (1, 1, 1), (1, -1, 5), (1, 2, 1),
             (2, 1, 2), (2, -1, 6), (2, -2, 3),
             (3, 1, 3), (3, -1, 7)]

    def from_hub(role):
        for n, (r, step, recv) in enumerate(nears):
            if r == role:
                near(r, step, n, recv).start()
        sib_copy(chunk_of(z + hub[role])).start()

    send_rows(t_ref, 8 * zh, (zh * 2 + c) * 16 + yx)

    @pl.when(away == 0)
    def _():
        drain(piv_ref.at[own_chunk], a2a_recv.at[0])
        for role in (1, 2, 3):
            piv_copy(own_chunk, z_dev(z + 16 - hub[role], yx, c), hub_send.at[role - 1], hub_recv.at[role - 1]).start()
        from_hub(0)
        for role in (1, 2):
            piv_copy(own_chunk, sib_dev, hub_send.at[role - 1], hub_recv.at[role - 1]).wait_recv()
            from_hub(role)

    to_mate.wait_recv()
    send_rows(mate_ref, 0, ((1 - zh) * 2 + c) * 16 + yx)

    @pl.when(away == 0)
    def _():
        piv_copy(own_chunk, sib_dev, hub_send.at[2], hub_recv.at[2]).wait_recv()
        from_hub(3)
        for recv, src in enumerate((-2, -6, 2, 6)):
            piv_copy(own_chunk, sib_dev, near_send.at[0], near_recv.at[recv]).wait_recv()
            sib_copy(chunk_of(z + src)).start()

    @pl.when(away == 1)
    def _():
        for role in range(4):
            for side in range(2):
                step = 1 - 2 * side
                piv_copy(own_chunk, sib_dev, near_send.at[0], near_recv.at[4 * side + role]).wait_recv()
                sib_copy(chunk_of(z - step + hub[role])).start()

    to_mate.wait_send()

    @pl.when(away == 0)
    def _():
        drain(t_ref.at[pl.ds(0, 7)], a2a_send.at[0])
        for role in (1, 2, 3):
            piv_copy(own_chunk, sib_dev, hub_send.at[role - 1], hub_recv.at[role - 1]).wait_send()
        for n in range(len(nears)):
            piv_copy(own_chunk, sib_dev, near_send.at[n], near_recv.at[0]).wait_send()

    @pl.when(away == 1)
    def _():
        drain(t_ref.at[pl.ds(0, 8)], a2a_send.at[0])

    drain(rows_ref.at[pl.ds(0, 62)], row_send.at[0])
    drain(piv_ref.at[pl.ds(0, 8)], sib_send.at[0])
    drain(rows_ref, row_recv.at[0])
    drain(piv_ref.at[pl.ds(0, 8)], sib_recv.at[0])

    block(rows_ref, piv_ref, part_ref, ag, ax, bg, bx, gg, xx, yx)

    slot = c * 16 + yx

    @pl.loop(1, 32)
    def _(i):
        yx2, c2 = plane_peer(a, i)
        remote(part_ref, parts.at[slot], send1.at[0], recv1.at[0], dev(k, yx2, zh, c2)).start()

    pltpu.make_async_copy(part_ref, parts.at[slot], recv1.at[0]).start()
    drain(parts, recv1.at[0])
    for c2 in range(2):
        plane_rows[pl.ds(c2 * 8, 8), :] = jnp.sum(parts[pl.ds(c2 * 16, 16)], axis=0)

    @pl.when(zh == 0)
    def _():
        @pl.loop(1, 16)
        def _(i):
            remote(plane_rows, diag_ref.at[k], send2.at[0], recv2.at[0], z_dev(z + i, yx, c)).start()

        pltpu.make_async_copy(plane_rows, diag_ref.at[k], recv2.at[0]).start()

    @pl.when(zh == 1)
    def _():
        remote(plane_rows, rest_ref, send2.at[0], recv3.at[0], mate_dev).start()
        pltpu.make_async_copy(plane_rows, rest_ref, recv3.at[0]).start()

    drain(diag_ref, recv2.at[0])
    drain(rest_ref, recv3.at[0])
    drain(parts.at[pl.ds(0, 31)], send1.at[0])

    @pl.when(zh == 0)
    def _():
        drain(parts.at[pl.ds(0, 30)], send2.at[0])

    @pl.when(zh == 1)
    def _():
        drain(plane_rows, send2.at[0])


def panel(order, x, g):
    dma = pltpu.SemaphoreType.DMA
    return pl.pallas_call(
        panel_kernel,
        out_shape=[jax.ShapeDtypeStruct((8, 16, 128), F32), jax.ShapeDtypeStruct((16, 128), F32)],
        in_specs=[SM, VM, VM],
        out_specs=[VM, VM],
        scratch_shapes=[
            pltpu.VMEM((128, 49), F32),
            pltpu.VMEM((128, 49), F32),
            pltpu.VMEM((16, 8, 128), F32),
            pltpu.VMEM((16, 16, 128), BF16),
            pltpu.VMEM((8, 16, 128), BF16),
            pltpu.VMEM((64, 4, 16, 128), BF16),
            pltpu.VMEM((16, 16, 16, 128), BF16),
        ]
        + [pltpu.VMEM((512, 512), BF16)] * 4
        + [pltpu.VMEM((512, 512), F32)] * 2
        + [pltpu.VMEM((8, 128), F32), pltpu.VMEM((32, 8, 128), F32), pltpu.VMEM((16, 128), F32)]
        + [dma((n,)) for n in (2, 1, 1, 1, 1, 3, 3, 12, 8, 1, 1, 1, 1, 1, 1, 1)],
        compiler_params=pltpu.CompilerParams(
            collective_id=0, has_side_effects=True, vmem_limit_bytes=32 * 1024 * 1024),
        name="panel",
    )(order, x, g)


def solve_kernel(diag_ref, rest_ref, ridge_ref, gram_ref, factor_ref):
    k, _, _, _ = place()
    gram_ref[pl.ds(0, 16), :] = diag_ref[k]
    gram_ref[pl.ds(16, 16), :] = rest_ref[...]
    gram = gram_ref[...]
    diag = diag_ref[...].reshape(128, 128)
    row = lax.broadcasted_iota(jnp.int32, (128, 128), 0)
    col = lax.broadcasted_iota(jnp.int32, (128, 128), 1)
    system = 0.5 * (diag + diag.T) + jnp.where(row == col, ridge_ref[...], 0.0)
    right = jnp.concatenate([gram, jnp.zeros((96, 128), F32)], axis=0).T
    sub = lax.broadcasted_iota(jnp.int32, (8, 128), 0)
    left = [system[8 * m:8 * m + 8] for m in range(16)]
    right = [right[8 * m:8 * m + 8] for m in range(16)]
    for j in range(128):
        m0, i = j // 8, j % 8
        pivot_row = left[m0][i:i + 1, :]
        right_row = right[m0][i:i + 1, :]
        pivot = left[m0][i:i + 1, j:j + 1]
        inverse = 1.0 / pivot
        scaled_row = pivot_row * inverse
        scaled_right = right_row * inverse
        for m in range(m0, 16):
            factor = jnp.broadcast_to(left[m][:, j:j + 1], (8, 128))
            if m == m0:
                factor = jnp.where(sub > i, factor, 0.0)
            left[m] = left[m] - factor * scaled_row
            right[m] = right[m] - factor * scaled_right
    lane = lax.broadcasted_iota(jnp.int32, (8, 128), 1)
    for m in range(16):
        pivots = jnp.sum(jnp.where(lane == sub + 8 * m, left[m], 0.0), axis=1, keepdims=True)
        right[m] = right[m] * lax.rsqrt(pivots)
    factor_ref[...] = jnp.concatenate(right, axis=0).T[:32]


def solve(diag, rest, ridge):
    out = jax.ShapeDtypeStruct((32, 128), F32)
    return pl.pallas_call(
        solve_kernel,
        out_shape=[out, out],
        in_specs=[VM, VM, VM],
        out_specs=[VM, VM],
        name="factor_solve",
    )(diag, rest, ridge)


def local(activations, cotangents, ordering, ridge):
    x = activations.transpose(1, 2, 3, 0).reshape(49, 8, 32)
    diag, rest = panel(ordering, x, cotangents)
    return tuple(solve(diag, rest, ridge.reshape(1, 128)))


def solution(mesh):
    return jax.shard_map(
        local,
        mesh=mesh,
        in_specs=(P("rows", None, None, "chan"), P("rows", "chan", None), P("rows", None), P()),
        out_specs=(P("rows", None), P("rows", None)),
        check_vma=False,
    )
```

time: 95.5 us -> 74.9 us (0.78)
  Pallas kernels: 93.1 us -> 70.4 us
  local copies, waits for them, and re-layouts: 1.44 us -> 3.58 us
    pallas_call x3 -> x0, Pallas kernels: 55.5 us -> none  [the longest x1 49.8 us: gather(): pl.pallas_call(gather_kernel, out_shape=[jax.ShapeDtypeStruct((64, 4, 16,...]
    pallas_call x1, Pallas kernels: 25.2 us -> 58 us  [panel(): pl.pallas_call(panel_kernel, out_shape=[jax.ShapeDtypeStruct((8, 16, 128)...]
    unnamed x4 -> x10, local copies, waits for them, and re-layouts: 1.44 us -> 3.58 us
where the time goes in v2:
time: 74.9 us; the launch traced here: 74.7 us
  Pallas kernels  70.4 us (94%)
  local copies, waits for them, and re-layouts  3.58 us (5%)
    pallas_call x1, Pallas kernels, panel(): pl.pallas_call(panel_kernel, out_shape=[jax.ShapeDtypeStruct((8, 16, 128)...  58 us
    pallas_call x1, Pallas kernels, solve(): pl.pallas_call(solve_kernel, out_shape=[out, out], in_specs=[VM, VM, VM],...  12.5 us
    unnamed x10, local copies, waits for them, and re-layouts  3.58 us

profile of v2, /device:TPU:1, one launch (start us, length us, event | category | flops | bytes accessed | tf_op | source)
XLA Modules:
  0.0 74.7 jit_solution(4059887556289919120)
XLA Ops:
  0.6 0.0 copy-start.4
  0.6 0.6 copy-done.4
  1.3 0.0 copy-start
  1.3 0.9 %copy-done = bf16[32,7,7,8]{0,3,2,1:T(8,128)(2,1)S(1)} copy-done((bf16[32,7,7,8]{0,3,2,1:T(8,128)(2,1)S(1)}, bf16[32,7,7,8]{0,3,2,1:T(8,128)(2,1)}, u32[]{:S(2)}) %copy-start) | copy-done | bytes 25112
  2.2 0.0 copy-start.2
  2.2 0.8 %copy-done.2 = bf16[32,8,49]{2,1,0:T(8,128)(2,1)S(1)} copy-done((bf16[32,8,49]{2,1,0:T(8,128)(2,1)S(1)}, bf16[32,8,49]{2,1,0:T(8,128)(2,1)}, u32[]{:S(2)}) %copy-start.2) | copy-done | bytes 25112
  3.0 58.0 %panel.1 = (f32[8,16,128]{2,1,0:T(8,128)S(1)}, f32[16,128]{1,0:T(8,128)S(1)}) custom-call(s32[1,32]{1,0:T(1,128)S(1)} %copy-done.4, bf16[49,8,32]{2,1,0:T(8,128)(2,1)S(1)} %bitcast.4, bf16[32,8,49]{2,1,0:T(8,128)(2,1)S(1)} %copy-done.2), custom_call_target="tpu_custom_call" | custom-call | tf_op jit(solution)/shard_map/panel/pallas_call | solution.py:289
  61.0 0.0 copy-start.1
  61.0 0.6 copy-done.1
  61.6 0.0 copy-start.3
  61.6 0.6 copy-done.3
  62.2 12.5 %factor_solve.1 = (f32[32,128]{1,0:T(8,128)}, f32[32,128]{1,0:T(8,128)}) custom-call(f32[8,16,128]{2,1,0:T(8,128)} %copy-done.1, f32[16,128]{1,0:T(8,128)} %copy-done.3, f32[1,128]{1,0:T(1,128)} %bitcast.5), custom_call_target="tpu_custom_call" | custom-call | tf_op jit(solution)/shard_map/factor_solve/pallas_call | solution.py:349
Async XLA Ops:
  0.6 0.7 copy-start.4
  1.3 0.9 %copy-start = (bf16[32,7,7,8]{0,3,2,1:T(8,128)(2,1)S(1)}, bf16[32,7,7,8]{0,3,2,1:T(8,128)(2,1)}, u32[]{:S(2)}) copy-start(bf16[32,7,7,8]{0,3,2,1:T(8,128)(2,1)} %param.4) | copy-start | bytes 75268
  2.2 0.8 %copy-start.2 = (bf16[32,8,49]{2,1,0:T(8,128)(2,1)S(1)}, bf16[32,8,49]{2,1,0:T(8,128)(2,1)}, u32[]{:S(2)}) copy-start(bf16[32,8,49]{2,1,0:T(8,128)(2,1)} %g_ref.1) | copy-start | bytes 75268
  61.0 0.6 copy-start.1
  61.6 0.6 copy-start.3

commit v3 on v2

--- a/solution.py
+++ b/solution.py
@@ -1,5 +1,3 @@
-import functools
-
 import jax
 import jax.numpy as jnp
 from jax import lax
@@ -11,7 +9,7 @@
 BF16 = jnp.bfloat16
 MESH = pl.DeviceIdType.MESH
 VM = pl.BlockSpec(memory_space=pltpu.VMEM)
-SM = pl.BlockSpec(memory_space=pltpu.SMEM)
+HBM = pl.BlockSpec(memory_space=pltpu.HBM)
 
 
 def place():
@@ -27,6 +25,10 @@
 def plane_peer(a, i):
     other = (a + i) % 32
     return other // 2, other % 2
+
+
+def far_first(i):
+    return 8 + (i // 2) * (1 - 2 * (i % 2))
 
 
 def z_dev(z, yx, c):
@@ -111,9 +113,64 @@
     out_ref[...] = pieces
 
 
-def panel_kernel(order_ref, x_ref, g_ref, diag_ref, rest_ref,
-                 ge, go, xs, t_ref, mate_ref, rows_ref, piv_ref, ag, ax, bg, bx, gg, xx, part_ref, parts, plane_rows,
-                 mate_sem, row_send, row_recv, a2a_send, a2a_recv, hub_send, hub_recv, near_send, near_recv,
+def eliminate(left, right, store):
+    full = (8, 128)
+    for m0 in range(16):
+        j0 = 8 * m0
+        rows = [jnp.broadcast_to(left[m0][i:i + 1, :], full) for i in range(8)]
+        rights = [jnp.broadcast_to(right[m0][i:i + 1, :], full) for i in range(8)]
+        cols = [jnp.broadcast_to(left[m0][:, j0 + l:j0 + l + 1], full) for l in range(8)]
+        e = [[jnp.broadcast_to(cols[l][i:i + 1, :], full) if i <= l else None for l in range(8)] for i in range(8)]
+        inverse, ratio = [], {}
+        for i in range(8):
+            inverse.append(1.0 / e[i][i])
+            for l in range(i + 1, 8):
+                ratio[i, l] = e[i][l] * inverse[i]
+            for l in range(i + 1, 8):
+                for n in range(l, 8):
+                    e[l][n] = e[l][n] - ratio[i, l] * e[i][n]
+                rows[l] = rows[l] - ratio[i, l] * rows[i]
+                rights[l] = rights[l] - ratio[i, l] * rights[i]
+        for i in range(8):
+            store(j0 + i, rights[i] * lax.rsqrt(e[i][i]))
+        if m0 == 15:
+            break
+        for i in reversed(range(8)):
+            rows[i] = rows[i] * inverse[i]
+            rights[i] = rights[i] * inverse[i]
+            for l in range(i + 1, 8):
+                rows[i] = rows[i] - ratio[i, l] * rows[l]
+                rights[i] = rights[i] - ratio[i, l] * rights[l]
+        for m in range(m0 + 1, 16):
+            block = left[m]
+            for i in range(8):
+                factor = jnp.broadcast_to(block[:, j0 + i:j0 + i + 1], full)
+                left[m] = left[m] - factor * rows[i]
+                right[m] = right[m] - factor * rights[i]
+
+
+def factor(panel_ref, ridge_ref, gram_ref, factor_ref, f_ref, k):
+    gram_ref[pl.ds(0, 16), :] = panel_ref[k]
+    gram_ref[pl.ds(16, 16), :] = panel_ref[8]
+    gram = gram_ref[...]
+    diag = panel_ref[0:8].reshape(128, 128)
+    row = lax.broadcasted_iota(jnp.int32, (128, 128), 0)
+    col = lax.broadcasted_iota(jnp.int32, (128, 128), 1)
+    system = 0.5 * (diag + diag.T) + jnp.where(row == col, ridge_ref[...], 0.0)
+    right = jnp.concatenate([gram, jnp.zeros((96, 128), F32)], axis=0).T
+    left = [system[8 * m:8 * m + 8] for m in range(16)]
+    right = [right[8 * m:8 * m + 8] for m in range(16)]
+
+    def store(row, values):
+        f_ref[pl.ds(row, 1), :] = values[0:1]
+
+    eliminate(left, right, store)
+    factor_ref[...] = f_ref[...].T[:32]
+
+
+def panel_kernel(order_hbm, x_hbm, g_hbm, ridge_hbm, gram_ref, factor_ref,
+                 out_ref, f_ref, ridge_ref, order_ref, x_ref, g_ref, ge, go, xs, t_ref, mate_ref, rows_ref, piv_ref, ag, ax, bg, bx, gg, xx, part_ref, parts, plane_rows,
+                 mate_sem, row_send, row_recv, piv_send, piv_recv, hop_send, in_sem,
                  sib_send, sib_recv, send1, recv1, send2, recv2, recv3):
     k, yx, zh, c = place()
     z = zh * 8 + k
@@ -124,17 +181,36 @@
 
     barrier = pltpu.get_barrier_semaphore()
 
+    def signal(target):
+        pl.semaphore_signal(barrier, inc=1, device_id=target, device_id_type=MESH)
+
+    @pl.loop(1, 16)
+    def _(i):
+        signal(z_dev(z + far_first(i), yx, c))
+
+    @pl.when(away == 1)
+    def _():
+        @pl.loop(0, 16)
+        def _(i):
+            signal(z_dev(z + 3, i, c))
+            signal(z_dev(z + 13, i, c))
+
+    operands = [
+        pltpu.make_async_copy(src, dst, in_sem.at[n])
+        for n, (src, dst) in enumerate(((order_hbm, order_ref), (x_hbm, x_ref), (g_hbm, g_ref), (ridge_hbm, ridge_ref)))
+    ]
+    for copy in operands:
+        copy.start()
+
     @pl.loop(1, 32)
     def _(i):
         yx2, c2 = plane_peer(a, i)
-        pl.semaphore_signal(barrier, inc=1, device_id=dev(k, yx2, zh, c2), device_id_type=MESH)
-
-    @pl.loop(1, 16)
-    def _(i):
-        pl.semaphore_signal(barrier, inc=1, device_id=z_dev(z + i, yx, c), device_id_type=MESH)
-
+        signal(dev(k, yx2, zh, c2))
+
+    for copy in operands:
+        copy.wait()
     lay_out(order_ref, x_ref, g_ref, t_ref, ge, go, xs, c)
-    pl.semaphore_wait(barrier, 46)
+    pl.semaphore_wait(barrier, 62)
 
     def remote(src, dst, send, recv, target):
         return pltpu.make_async_remote_copy(
@@ -151,17 +227,22 @@
         return (((src_z % 8) // 2) * 2 + src_z // 8) * 2 + c
 
     own_chunk = chunk_of(z)
-    for u in range(8):
-        target = (u // 2) * 4 + 2 * (u % 2) + k % 2
-
-        @pl.when(target == yx)
-        def _():
-            pltpu.make_async_copy(t_ref.at[u], piv_ref.at[own_chunk, yx], a2a_recv.at[0]).start()
-
-        @pl.when(target != yx)
-        def _():
-            remote(t_ref.at[u], piv_ref.at[own_chunk, yx], a2a_send.at[0], a2a_recv.at[0],
-                   dev(k, target, zh, c)).start()
+    for step in (3, 13, 0):
+        for u in range(8):
+            target = (u // 2) * 4 + 2 * (u % 2) + k % 2
+            recv = piv_recv.at[{3: 3, 13: 13, 0: 0}[step]]
+            tile = remote(t_ref.at[u], piv_ref.at[own_chunk, yx], piv_send.at[0], recv, z_dev(z + step, target, c))
+            if step:
+                tile.start()
+                continue
+
+            @pl.when(target == yx)
+            def _():
+                pltpu.make_async_copy(t_ref.at[u], piv_ref.at[own_chunk, yx], recv).start()
+
+            @pl.when(target != yx)
+            def _():
+                tile.start()
 
     def send_rows(src_ref, base, slot):
         @pl.loop(1, 32)
@@ -178,66 +259,53 @@
     def sib_copy(chunk):
         return piv_copy(chunk, sib_dev, sib_send.at[0], sib_recv.at[0])
 
-    hub = (0, -4, 4, 8)
-
-    def near(role, step, n, recv):
-        return piv_copy(chunk_of(z + hub[role]), z_dev(z + 16 + step, yx, c), near_send.at[n], near_recv.at[recv])
-
-    nears = [(0, 1, 0), (0, -1, 4), (0, 2, 0), (0, -2, 2),
-             (1, 1, 1), (1, -1, 5), (1, 2, 1),
-             (2, 1, 2), (2, -1, 6), (2, -2, 3),
-             (3, 1, 3), (3, -1, 7)]
-
-    def from_hub(role):
-        for n, (r, step, recv) in enumerate(nears):
-            if r == role:
-                near(r, step, n, recv).start()
-        sib_copy(chunk_of(z + hub[role])).start()
+    def hop(off, step):
+        return piv_copy(chunk_of(z - off), z_dev(z + 16 + step, yx, c), hop_send.at[0], piv_recv.at[(off + step) % 16])
+
+    def arrived(off, steps=()):
+        drain(piv_ref.at[chunk_of(z - off)], piv_recv.at[off % 16])
+        for step in steps:
+            hop(off, step).start()
+        sib_copy(chunk_of(z - off)).start()
 
     send_rows(t_ref, 8 * zh, (zh * 2 + c) * 16 + yx)
 
     @pl.when(away == 0)
     def _():
-        drain(piv_ref.at[own_chunk], a2a_recv.at[0])
-        for role in (1, 2, 3):
-            piv_copy(own_chunk, z_dev(z + 16 - hub[role], yx, c), hub_send.at[role - 1], hub_recv.at[role - 1]).start()
-        from_hub(0)
-        for role in (1, 2):
-            piv_copy(own_chunk, sib_dev, hub_send.at[role - 1], hub_recv.at[role - 1]).wait_recv()
-            from_hub(role)
+        arrived(0, (1, -1))
+
+    @pl.when(away == 1)
+    def _():
+        arrived(3, (3, 1, -1))
+        arrived(-3, (-3, -1, 1))
 
     to_mate.wait_recv()
     send_rows(mate_ref, 0, ((1 - zh) * 2 + c) * 16 + yx)
 
     @pl.when(away == 0)
     def _():
-        piv_copy(own_chunk, sib_dev, hub_send.at[2], hub_recv.at[2]).wait_recv()
-        from_hub(3)
-        for recv, src in enumerate((-2, -6, 2, 6)):
-            piv_copy(own_chunk, sib_dev, near_send.at[0], near_recv.at[recv]).wait_recv()
-            sib_copy(chunk_of(z + src)).start()
+        arrived(6, (2, 1, -1))
+        arrived(-6, (-1, 1))
+        for off in (2, -2, 4, -4, 8):
+            arrived(off)
 
     @pl.when(away == 1)
     def _():
-        for role in range(4):
-            for side in range(2):
-                step = 1 - 2 * side
-                piv_copy(own_chunk, sib_dev, near_send.at[0], near_recv.at[4 * side + role]).wait_recv()
-                sib_copy(chunk_of(z - step + hub[role])).start()
+        for off in (1, -1, 5, -5, 7, -7):
+            arrived(off)
 
     to_mate.wait_send()
 
     @pl.when(away == 0)
     def _():
-        drain(t_ref.at[pl.ds(0, 7)], a2a_send.at[0])
-        for role in (1, 2, 3):
-            piv_copy(own_chunk, sib_dev, hub_send.at[role - 1], hub_recv.at[role - 1]).wait_send()
-        for n in range(len(nears)):
-            piv_copy(own_chunk, sib_dev, near_send.at[n], near_recv.at[0]).wait_send()
+        drain(rows_ref.at[pl.ds(0, 5)], piv_send.at[0])
+        drain(rows_ref.at[pl.ds(0, 3), pl.ds(0, 1)], piv_send.at[0])
+        drain(piv_ref.at[pl.ds(0, 7)], hop_send.at[0])
 
     @pl.when(away == 1)
     def _():
-        drain(t_ref.at[pl.ds(0, 8)], a2a_send.at[0])
+        drain(rows_ref.at[pl.ds(0, 6)], piv_send.at[0])
+        drain(piv_ref.at[pl.ds(0, 6)], hop_send.at[0])
 
     drain(rows_ref.at[pl.ds(0, 62)], row_send.at[0])
     drain(piv_ref.at[pl.ds(0, 8)], sib_send.at[0])
@@ -262,17 +330,18 @@
     def _():
         @pl.loop(1, 16)
         def _(i):
-            remote(plane_rows, diag_ref.at[k], send2.at[0], recv2.at[0], z_dev(z + i, yx, c)).start()
-
-        pltpu.make_async_copy(plane_rows, diag_ref.at[k], recv2.at[0]).start()
+            remote(plane_rows, out_ref.at[k], send2.at[0], recv2.at[0], z_dev(z + far_first(i), yx, c)).start()
+
+        pltpu.make_async_copy(plane_rows, out_ref.at[k], recv2.at[0]).start()
 
     @pl.when(zh == 1)
     def _():
-        remote(plane_rows, rest_ref, send2.at[0], recv3.at[0], mate_dev).start()
-        pltpu.make_async_copy(plane_rows, rest_ref, recv3.at[0]).start()
-
-    drain(diag_ref, recv2.at[0])
-    drain(rest_ref, recv3.at[0])
+        remote(plane_rows, out_ref.at[8], send2.at[0], recv3.at[0], mate_dev).start()
+        pltpu.make_async_copy(plane_rows, out_ref.at[8], recv3.at[0]).start()
+
+    drain(out_ref.at[pl.ds(0, 8)], recv2.at[0])
+    drain(out_ref.at[8], recv3.at[0])
+    factor(out_ref, ridge_ref, gram_ref, factor_ref, f_ref, k)
     drain(parts.at[pl.ds(0, 31)], send1.at[0])
 
     @pl.when(zh == 0)
@@ -284,14 +353,21 @@
         drain(plane_rows, send2.at[0])
 
 
-def panel(order, x, g):
+def panel(order, x, g, ridge):
+    out = jax.ShapeDtypeStruct((32, 128), F32)
     dma = pltpu.SemaphoreType.DMA
     return pl.pallas_call(
         panel_kernel,
-        out_shape=[jax.ShapeDtypeStruct((8, 16, 128), F32), jax.ShapeDtypeStruct((16, 128), F32)],
-        in_specs=[SM, VM, VM],
+        out_shape=[out, out],
+        in_specs=[HBM] * 4,
         out_specs=[VM, VM],
         scratch_shapes=[
+            pltpu.VMEM((9, 16, 128), F32),
+            pltpu.VMEM((128, 128), F32),
+            pltpu.VMEM((1, 128), F32),
+            pltpu.SMEM((1, 32), jnp.int32),
+            pltpu.VMEM((49, 8, 32), BF16),
+            pltpu.VMEM((32, 8, 49), BF16),
             pltpu.VMEM((128, 49), F32),
             pltpu.VMEM((128, 49), F32),
             pltpu.VMEM((16, 8, 128), F32),
@@ -303,62 +379,16 @@
         + [pltpu.VMEM((512, 512), BF16)] * 4
         + [pltpu.VMEM((512, 512), F32)] * 2
         + [pltpu.VMEM((8, 128), F32), pltpu.VMEM((32, 8, 128), F32), pltpu.VMEM((16, 128), F32)]
-        + [dma((n,)) for n in (2, 1, 1, 1, 1, 3, 3, 12, 8, 1, 1, 1, 1, 1, 1, 1)],
+        + [dma((n,)) for n in (2, 1, 1, 1, 16, 1, 4, 1, 1, 1, 1, 1, 1, 1)],
         compiler_params=pltpu.CompilerParams(
-            collective_id=0, has_side_effects=True, vmem_limit_bytes=32 * 1024 * 1024),
+            collective_id=0, has_side_effects=True, vmem_limit_bytes=56 * 1024 * 1024),
         name="panel",
-    )(order, x, g)
-
-
-def solve_kernel(diag_ref, rest_ref, ridge_ref, gram_ref, factor_ref):
-    k, _, _, _ = place()
-    gram_ref[pl.ds(0, 16), :] = diag_ref[k]
-    gram_ref[pl.ds(16, 16), :] = rest_ref[...]
-    gram = gram_ref[...]
-    diag = diag_ref[...].reshape(128, 128)
-    row = lax.broadcasted_iota(jnp.int32, (128, 128), 0)
-    col = lax.broadcasted_iota(jnp.int32, (128, 128), 1)
-    system = 0.5 * (diag + diag.T) + jnp.where(row == col, ridge_ref[...], 0.0)
-    right = jnp.concatenate([gram, jnp.zeros((96, 128), F32)], axis=0).T
-    sub = lax.broadcasted_iota(jnp.int32, (8, 128), 0)
-    left = [system[8 * m:8 * m + 8] for m in range(16)]
-    right = [right[8 * m:8 * m + 8] for m in range(16)]
-    for j in range(128):
-        m0, i = j // 8, j % 8
-        pivot_row = left[m0][i:i + 1, :]
-        right_row = right[m0][i:i + 1, :]
-        pivot = left[m0][i:i + 1, j:j + 1]
-        inverse = 1.0 / pivot
-        scaled_row = pivot_row * inverse
-        scaled_right = right_row * inverse
-        for m in range(m0, 16):
-            factor = jnp.broadcast_to(left[m][:, j:j + 1], (8, 128))
-            if m == m0:
-                factor = jnp.where(sub > i, factor, 0.0)
-            left[m] = left[m] - factor * scaled_row
-            right[m] = right[m] - factor * scaled_right
-    lane = lax.broadcasted_iota(jnp.int32, (8, 128), 1)
-    for m in range(16):
-        pivots = jnp.sum(jnp.where(lane == sub + 8 * m, left[m], 0.0), axis=1, keepdims=True)
-        right[m] = right[m] * lax.rsqrt(pivots)
-    factor_ref[...] = jnp.concatenate(right, axis=0).T[:32]
-
-
-def solve(diag, rest, ridge):
-    out = jax.ShapeDtypeStruct((32, 128), F32)
-    return pl.pallas_call(
-        solve_kernel,
-        out_shape=[out, out],
-        in_specs=[VM, VM, VM],
-        out_specs=[VM, VM],
-        name="factor_solve",
-    )(diag, rest, ridge)
+    )(order, x, g, ridge)
 
 
 def local(activations, cotangents, ordering, ridge):
     x = activations.transpose(1, 2, 3, 0).reshape(49, 8, 32)
-    diag, rest = panel(ordering, x, cotangents)
-    return tuple(solve(diag, rest, ridge.reshape(1, 128)))
+    return tuple(panel(ordering, x, cotangents, ridge.reshape(1, 128)))
 
 
 def solution(mesh):

time: 74.9 us -> 64.2 us (0.86)
  Pallas kernels: 70.4 us -> 61.4 us
  local copies, waits for them, and re-layouts: 3.58 us -> 1.94 us
    pallas_call x2 -> x1, Pallas kernels: 70.4 us -> 61.4 us  [panel(): pl.pallas_call(panel_kernel, out_shape=[out, out], in_specs=[HBM] * 4, ou...]
    unnamed x10 -> x4, local copies, waits for them, and re-layouts: 3.58 us -> 1.94 us
where the time goes in v3:
time: 64.2 us; the launch traced here: 64 us
  Pallas kernels  61.4 us (96%)
  local copies, waits for them, and re-layouts  1.94 us (3%)
  between operations  0.65 us (1%)
    pallas_call x1, Pallas kernels, panel(): pl.pallas_call(panel_kernel, out_shape=[out, out], in_specs=[HBM] * 4, ou...  61.4 us
    unnamed x4, local copies, waits for them, and re-layouts  1.94 us

profile of v3, /device:TPU:1, one launch (start us, length us, event | category | flops | bytes accessed | tf_op | source)
XLA Modules:
  0.0 64.0 jit_solution(1863795362409991598)
XLA Ops:
  0.6 61.4 %panel.1 = (f32[32,128]{1,0:T(8,128)}, f32[32,128]{1,0:T(8,128)}) custom-call(s32[1,32]{1,0:T(1,128)} %order_hbm.1, bf16[49,8,32]{2,1,0:T(8,128)(2,1)} %bitcast.4, bf16[32,8,49]{2,1,0:T(8,128)(2,1)} %g_hbm.1, f32[1,128]{1,0:T(1,128)} %bitcast.5), custom_call_target="tpu_custom_call" | custom-call | tf_op jit(solution)/shard_map/panel/pallas_call | solution.py:359
  62.0 0.0 copy-start
  62.0 1.3 %copy.8 = f32[32,128]{1,0:T(8,128)} copy(f32[32,128]{1,0:T(8,128)} %get-tuple-element.4) | data formatting | bytes 32768
  63.3 0.0 copy-done
  63.3 0.6 copy.9
Async XLA Ops:
  62.0 1.3 %copy-start = (f32[32,128]{1,0:T(8,128)S(1)}, f32[32,128]{1,0:T(8,128)}, u32[]{:S(2)}) copy-start(f32[32,128]{1,0:T(8,128)} %get-tuple-element.5) | copy-start | bytes 49156

commit v4 on v3

--- a/solution.py
+++ b/solution.py
@@ -22,9 +22,13 @@
     return {"rows": k, "chan": (yx * 2 + zh) * 2 + c}
 
 
-def plane_peer(a, i):
-    other = (a + i) % 32
-    return other // 2, other % 2
+def plane_peers(yx, c):
+    steps = sorted(((dy, dx) for dy in range(4) for dx in range(4)),
+                   key=lambda step: -sum(min(d, 4 - d) for d in step))
+    for dy, dx in steps:
+        for flip in (0, 1):
+            if dy or dx or flip:
+                yield ((yx // 4 + dy) % 4) * 4 + (yx + dx) % 4, (c + flip) % 2
 
 
 def far_first(i):
@@ -168,13 +172,12 @@
     factor_ref[...] = f_ref[...].T[:32]
 
 
-def panel_kernel(order_hbm, x_hbm, g_hbm, ridge_hbm, gram_ref, factor_ref,
+def panel_kernel(order_hbm, x_hbm, g_hbm, ridge_hbm, both_ref,
                  out_ref, f_ref, ridge_ref, order_ref, x_ref, g_ref, ge, go, xs, t_ref, mate_ref, rows_ref, piv_ref, ag, ax, bg, bx, gg, xx, part_ref, parts, plane_rows,
                  mate_sem, row_send, row_recv, piv_send, piv_recv, hop_send, in_sem,
                  sib_send, sib_recv, send1, recv1, send2, recv2, recv3):
     k, yx, zh, c = place()
     z = zh * 8 + k
-    a = yx * 2 + c
     away = (k + yx) % 2
     mate_dev = dev(k, yx, 1 - zh, c)
     sib_dev = dev(k, yx, zh, 1 - c)
@@ -202,9 +205,7 @@
     for copy in operands:
         copy.start()
 
-    @pl.loop(1, 32)
-    def _(i):
-        yx2, c2 = plane_peer(a, i)
+    for yx2, c2 in plane_peers(yx, c):
         signal(dev(k, yx2, zh, c2))
 
     for copy in operands:
@@ -220,7 +221,6 @@
         pltpu.make_async_copy(ref, ref, sem).wait()
 
     to_mate = remote(t_ref.at[pl.ds(8 * (1 - zh), 8)], mate_ref, mate_sem.at[0], mate_sem.at[1], mate_dev)
-    to_mate.start()
 
     def chunk_of(src_z):
         src_z = (src_z + 32) % 16
@@ -245,9 +245,7 @@
                 tile.start()
 
     def send_rows(src_ref, base, slot):
-        @pl.loop(1, 32)
-        def _(i):
-            yx2, c2 = plane_peer(a, i)
+        for yx2, c2 in plane_peers(yx, c):
             remote(src_ref.at[pl.ds(base + 4 * c2, 4)], rows_ref.at[slot], row_send.at[0], row_recv.at[0],
                    dev(k, yx2, zh, c2)).start()
 
@@ -268,6 +266,7 @@
             hop(off, step).start()
         sib_copy(chunk_of(z - off)).start()
 
+    to_mate.start()
     send_rows(t_ref, 8 * zh, (zh * 2 + c) * 16 + yx)
 
     @pl.when(away == 0)
@@ -316,9 +315,7 @@
 
     slot = c * 16 + yx
 
-    @pl.loop(1, 32)
-    def _(i):
-        yx2, c2 = plane_peer(a, i)
+    for yx2, c2 in plane_peers(yx, c):
         remote(part_ref, parts.at[slot], send1.at[0], recv1.at[0], dev(k, yx2, zh, c2)).start()
 
     pltpu.make_async_copy(part_ref, parts.at[slot], recv1.at[0]).start()
@@ -341,7 +338,7 @@
 
     drain(out_ref.at[pl.ds(0, 8)], recv2.at[0])
     drain(out_ref.at[8], recv3.at[0])
-    factor(out_ref, ridge_ref, gram_ref, factor_ref, f_ref, k)
+    factor(out_ref, ridge_ref, both_ref.at[0], both_ref.at[1], f_ref, k)
     drain(parts.at[pl.ds(0, 31)], send1.at[0])
 
     @pl.when(zh == 0)
@@ -354,13 +351,12 @@
 
 
 def panel(order, x, g, ridge):
-    out = jax.ShapeDtypeStruct((32, 128), F32)
     dma = pltpu.SemaphoreType.DMA
     return pl.pallas_call(
         panel_kernel,
-        out_shape=[out, out],
+        out_shape=jax.ShapeDtypeStruct((2, 32, 128), F32),
         in_specs=[HBM] * 4,
-        out_specs=[VM, VM],
+        out_specs=VM,
         scratch_shapes=[
             pltpu.VMEM((9, 16, 128), F32),
             pltpu.VMEM((128, 128), F32),
@@ -388,7 +384,8 @@
 
 def local(activations, cotangents, ordering, ridge):
     x = activations.transpose(1, 2, 3, 0).reshape(49, 8, 32)
-    return tuple(panel(ordering, x, cotangents, ridge.reshape(1, 128)))
+    both = panel(ordering, x, cotangents, ridge.reshape(1, 128))
+    return both[0], both[1]
 
 
 def solution(mesh):

time: 64.2 us -> 62.3 us (0.970)
  Pallas kernels: 61.4 us -> 60.1 us
    unnamed x4 -> x0, local copies, waits for them, and re-layouts: 1.94 us -> none
    squeeze x0 -> x1, local copies, waits for them, and re-layouts: none -> 1.35 us  [local(): return (both[0], both[1])]
    pallas_call x1, Pallas kernels: 61.4 us -> 60.1 us  [panel(): pl.pallas_call(panel_kernel, out_shape=jax.ShapeDtypeStruct((2, 32, 128),...]
where the time goes in v4:
time: 62.3 us; the launch traced here: 62.1 us
  Pallas kernels  60.1 us (96%)
  local copies, waits for them, and re-layouts  1.35 us (2%)
  between operations  0.64 us (1%)
    pallas_call x1, Pallas kernels, panel(): pl.pallas_call(panel_kernel, out_shape=jax.ShapeDtypeStruct((2, 32, 128),...  60.1 us
    squeeze x1, local copies, waits for them, and re-layouts, local(): return (both[0], both[1])  1.35 us

profile of v4, /device:TPU:1, one launch (start us, length us, event | category | flops | bytes accessed | tf_op | source)
XLA Modules:
  0.0 62.1 jit_solution(616607135675124252)
XLA Ops:
  0.6 60.1 %panel.1 = f32[2,32,128]{2,1,0:T(8,128)} custom-call(s32[1,32]{1,0:T(1,128)} %order_hbm.1, bf16[49,8,32]{2,1,0:T(8,128)(2,1)} %bitcast.8, bf16[32,8,49]{2,1,0:T(8,128)(2,1)} %g_hbm.1, f32[1,128]{1,0:T(1,128)} %bitcast.9), custom_call_target="tpu_custom_call" | custom-call | tf_op jit(solution)/shard_map/panel/pallas_call | solution.py:355
  60.7 1.3 %slice_bitcast_fusion = (f32[32,128]{1,0:T(8,128)}, f32[32,128]{1,0:T(8,128)}) fusion(f32[2,32,128]{2,1,0:T(8,128)} %panel.1), kind=kLoop, calls=%fused_computation | loop fusion | bytes 65536 | tf_op jit(solution)/shard_map/squeeze | solution.py:388

commit v5 on v4

--- a/solution.py
+++ b/solution.py
@@ -76,18 +76,24 @@
     out_ref[...] = jnp.concatenate([first, second], axis=1).astype(BF16)
 
 
-def block(rows_ref, piv_ref, out_ref, ag, ax, bg, bx, gg, xx, yx):
+def split(z2, u, even, odd, grads, inputs):
     mask = lax.broadcasted_iota(jnp.int32, (16, 16, 128), 1) < 8
+    at = pl.ds(z2 * 256, 256), pl.ds(u * 128, 128)
+    grads[at] = jnp.where(mask, even, odd).reshape(256, 128)
+    inputs[at] = jnp.where(mask, odd, even).reshape(256, 128)
+
+
+def split_rows(rows_ref, ag, ax):
     for z2 in range(2):
         for u in range(4):
-            even = rows_ref[pl.ds(z2 * 32, 16), u]
-            odd = rows_ref[pl.ds(z2 * 32 + 16, 16), u]
-            ag[pl.ds(z2 * 256, 256), pl.ds(u * 128, 128)] = jnp.where(mask, even, odd).reshape(256, 128)
-            ax[pl.ds(z2 * 256, 256), pl.ds(u * 128, 128)] = jnp.where(mask, odd, even).reshape(256, 128)
-            even = piv_ref[(u * 2 + z2) * 2]
-            odd = piv_ref[(u * 2 + z2) * 2 + 1]
-            bg[pl.ds(z2 * 256, 256), pl.ds(u * 128, 128)] = jnp.where(mask, even, odd).reshape(256, 128)
-            bx[pl.ds(z2 * 256, 256), pl.ds(u * 128, 128)] = jnp.where(mask, odd, even).reshape(256, 128)
+            split(z2, u, rows_ref[pl.ds(z2 * 32, 16), u], rows_ref[pl.ds(z2 * 32 + 16, 16), u], ag, ax)
+
+
+def block(piv_ref, out_ref, ag, ax, bg, bx, gg, xx, yx):
+    for z2 in range(2):
+        for u in range(4):
+            chunk = (u * 2 + z2) * 2
+            split(z2, u, piv_ref[chunk], piv_ref[chunk + 1], bg, bx)
     dims = (((0,), (0,)), ((), ()))
     gg[...] = lax.dot_general(ag[...], bg[...], dims, preferred_element_type=F32)
     xx[...] = lax.dot_general(ax[...], bx[...], dims, preferred_element_type=F32)
@@ -146,11 +152,12 @@
                 rows[i] = rows[i] - ratio[i, l] * rows[l]
                 rights[i] = rights[i] - ratio[i, l] * rights[l]
         for m in range(m0 + 1, 16):
-            block = left[m]
-            for i in range(8):
-                factor = jnp.broadcast_to(block[:, j0 + i:j0 + i + 1], full)
-                left[m] = left[m] - factor * rows[i]
-                right[m] = right[m] - factor * rights[i]
+            factors = [jnp.broadcast_to(left[m][:, j0 + i:j0 + i + 1], full) for i in range(8)]
+            for side, vectors in ((left, rows), (right, rights)):
+                terms = [f * v for f, v in zip(factors, vectors)]
+                while len(terms) > 1:
+                    terms = [terms[n] + terms[n + 1] for n in range(0, len(terms), 2)]
+                side[m] = side[m] - terms[0]
 
 
 def factor(panel_ref, ridge_ref, gram_ref, factor_ref, f_ref, k):
@@ -293,25 +300,10 @@
         for off in (1, -1, 5, -5, 7, -7):
             arrived(off)
 
-    to_mate.wait_send()
-
-    @pl.when(away == 0)
-    def _():
-        drain(rows_ref.at[pl.ds(0, 5)], piv_send.at[0])
-        drain(rows_ref.at[pl.ds(0, 3), pl.ds(0, 1)], piv_send.at[0])
-        drain(piv_ref.at[pl.ds(0, 7)], hop_send.at[0])
-
-    @pl.when(away == 1)
-    def _():
-        drain(rows_ref.at[pl.ds(0, 6)], piv_send.at[0])
-        drain(piv_ref.at[pl.ds(0, 6)], hop_send.at[0])
-
-    drain(rows_ref.at[pl.ds(0, 62)], row_send.at[0])
-    drain(piv_ref.at[pl.ds(0, 8)], sib_send.at[0])
     drain(rows_ref, row_recv.at[0])
+    split_rows(rows_ref, ag, ax)
     drain(piv_ref.at[pl.ds(0, 8)], sib_recv.at[0])
-
-    block(rows_ref, piv_ref, part_ref, ag, ax, bg, bx, gg, xx, yx)
+    block(piv_ref, part_ref, ag, ax, bg, bx, gg, xx, yx)
 
     slot = c * 16 + yx
 
@@ -336,6 +328,21 @@
         remote(plane_rows, out_ref.at[8], send2.at[0], recv3.at[0], mate_dev).start()
         pltpu.make_async_copy(plane_rows, out_ref.at[8], recv3.at[0]).start()
 
+    to_mate.wait_send()
+
+    @pl.when(away == 0)
+    def _():
+        drain(rows_ref.at[pl.ds(0, 5)], piv_send.at[0])
+        drain(rows_ref.at[pl.ds(0, 3), pl.ds(0, 1)], piv_send.at[0])
+        drain(piv_ref.at[pl.ds(0, 7)], hop_send.at[0])
+
+    @pl.when(away == 1)
+    def _():
+        drain(rows_ref.at[pl.ds(0, 6)], piv_send.at[0])
+        drain(piv_ref.at[pl.ds(0, 6)], hop_send.at[0])
+
+    drain(rows_ref.at[pl.ds(0, 62)], row_send.at[0])
+    drain(piv_ref.at[pl.ds(0, 8)], sib_send.at[0])
     drain(out_ref.at[pl.ds(0, 8)], recv2.at[0])
     drain(out_ref.at[8], recv3.at[0])
     factor(out_ref, ridge_ref, both_ref.at[0], both_ref.at[1], f_ref, k)

time: 62.3 us -> 61.4 us (0.986)
  Pallas kernels: 60.1 us -> 59.2 us
    pallas_call x1, Pallas kernels: 60.1 us -> 59.2 us  [panel(): pl.pallas_call(panel_kernel, out_shape=jax.ShapeDtypeStruct((2, 32, 128),...]
where the time goes in v5:
time: 61.4 us; the launch traced here: 61.2 us
  Pallas kernels  59.2 us (96%)
  local copies, waits for them, and re-layouts  1.35 us (2%)
  between operations  0.64 us (1%)
    pallas_call x1, Pallas kernels, panel(): pl.pallas_call(panel_kernel, out_shape=jax.ShapeDtypeStruct((2, 32, 128),...  59.2 us
    squeeze x1, local copies, waits for them, and re-layouts, local(): return (both[0], both[1])  1.35 us

profile of v5, /device:TPU:1, one launch (start us, length us, event | category | flops | bytes accessed | tf_op | source)
XLA Modules:
  0.0 61.2 jit_solution(8023569498109836114)
XLA Ops:
  0.6 59.2 %panel.1 = f32[2,32,128]{2,1,0:T(8,128)} custom-call(s32[1,32]{1,0:T(1,128)} %order_hbm.1, bf16[49,8,32]{2,1,0:T(8,128)(2,1)} %bitcast.8, bf16[32,8,49]{2,1,0:T(8,128)(2,1)} %g_hbm.1, f32[1,128]{1,0:T(1,128)} %bitcast.9), custom_call_target="tpu_custom_call" | custom-call | tf_op jit(solution)/shard_map/panel/pallas_call | solution.py:362
  59.8 1.3 %slice_bitcast_fusion = (f32[32,128]{1,0:T(8,128)}, f32[32,128]{1,0:T(8,128)}) fusion(f32[2,32,128]{2,1,0:T(8,128)} %panel.1), kind=kLoop, calls=%fused_computation | loop fusion | bytes 65536 | tf_op jit(solution)/shard_map/squeeze | solution.py:395

commit v6 on v5

--- a/solution.py
+++ b/solution.py
@@ -133,7 +133,9 @@
         e = [[jnp.broadcast_to(cols[l][i:i + 1, :], full) if i <= l else None for l in range(8)] for i in range(8)]
         inverse, ratio = [], {}
         for i in range(8):
-            inverse.append(1.0 / e[i][i])
+            if i % 2 == 0:
+                inverse.append(1.0 / e[i][i])
+                inverse.append(e[i][i] / (e[i][i] * e[i + 1][i + 1] - e[i][i + 1] * e[i][i + 1]))
             for l in range(i + 1, 8):
                 ratio[i, l] = e[i][l] * inverse[i]
             for l in range(i + 1, 8):
@@ -148,7 +150,7 @@
         for i in reversed(range(8)):
             rows[i] = rows[i] * inverse[i]
             rights[i] = rights[i] * inverse[i]
-            for l in range(i + 1, 8):
+            for l in reversed(range(i + 1, 8)):
                 rows[i] = rows[i] - ratio[i, l] * rows[l]
                 rights[i] = rights[i] - ratio[i, l] * rights[l]
         for m in range(m0 + 1, 16):

time: 61.4 us -> 60.1 us (0.979)
  Pallas kernels: 59.2 us -> 57.9 us
    pallas_call x1, Pallas kernels: 59.2 us -> 57.9 us  [panel(): pl.pallas_call(panel_kernel, out_shape=jax.ShapeDtypeStruct((2, 32, 128),...]
where the time goes in v6:
time: 60.1 us; the launch traced here: 59.9 us
  Pallas kernels  57.9 us (96%)
  local copies, waits for them, and re-layouts  1.35 us (2%)
  between operations  0.64 us (1%)
    pallas_call x1, Pallas kernels, panel(): pl.pallas_call(panel_kernel, out_shape=jax.ShapeDtypeStruct((2, 32, 128),...  57.9 us
    squeeze x1, local copies, waits for them, and re-layouts, local(): return (both[0], both[1])  1.35 us

profile of v6, /device:TPU:1, one launch (start us, length us, event | category | flops | bytes accessed | tf_op | source)
XLA Modules:
  0.0 59.9 jit_solution(8989802074500360735)
XLA Ops:
  0.6 57.9 %panel.1 = f32[2,32,128]{2,1,0:T(8,128)} custom-call(s32[1,32]{1,0:T(1,128)} %order_hbm.1, bf16[49,8,32]{2,1,0:T(8,128)(2,1)} %bitcast.8, bf16[32,8,49]{2,1,0:T(8,128)(2,1)} %g_hbm.1, f32[1,128]{1,0:T(1,128)} %bitcast.9), custom_call_target="tpu_custom_call" | custom-call | tf_op jit(solution)/shard_map/panel/pallas_call | solution.py:364
  58.5 1.3 %slice_bitcast_fusion = (f32[32,128]{1,0:T(8,128)}, f32[32,128]{1,0:T(8,128)}) fusion(f32[2,32,128]{2,1,0:T(8,128)} %panel.1), kind=kLoop, calls=%fused_computation | loop fusion | bytes 65536 | tf_op jit(solution)/shard_map/squeeze | solution.py:397

commit v7 on v6

--- a/solution.py
+++ b/solution.py
@@ -131,7 +131,7 @@
         rights = [jnp.broadcast_to(right[m0][i:i + 1, :], full) for i in range(8)]
         cols = [jnp.broadcast_to(left[m0][:, j0 + l:j0 + l + 1], full) for l in range(8)]
         e = [[jnp.broadcast_to(cols[l][i:i + 1, :], full) if i <= l else None for l in range(8)] for i in range(8)]
-        inverse, ratio = [], {}
+        inverse, ratio, unit = [], {}, {}
         for i in range(8):
             if i % 2 == 0:
                 inverse.append(1.0 / e[i][i])
@@ -141,18 +141,26 @@
             for l in range(i + 1, 8):
                 for n in range(l, 8):
                     e[l][n] = e[l][n] - ratio[i, l] * e[i][n]
+                unit[l, i] = -ratio[i, l]
+                for n in range(i):
+                    unit[l, n] = unit[l, n] - ratio[i, l] * unit[i, n]
                 rows[l] = rows[l] - ratio[i, l] * rows[i]
                 rights[l] = rights[l] - ratio[i, l] * rights[i]
         for i in range(8):
             store(j0 + i, rights[i] * lax.rsqrt(e[i][i]))
         if m0 == 15:
             break
-        for i in reversed(range(8)):
-            rows[i] = rows[i] * inverse[i]
-            rights[i] = rights[i] * inverse[i]
-            for l in reversed(range(i + 1, 8)):
-                rows[i] = rows[i] - ratio[i, l] * rows[l]
-                rights[i] = rights[i] - ratio[i, l] * rights[l]
+        rows = [row * scale for row, scale in zip(rows, inverse)]
+        rights = [row * scale for row, scale in zip(rights, inverse)]
+
+        def back(vectors, i):
+            terms = [vectors[i]] + [unit[l, i] * vectors[l] for l in range(i + 1, 8)]
+            while len(terms) > 1:
+                terms = [sum(terms[n + 1:n + 2], terms[n]) for n in range(0, len(terms), 2)]
+            return terms[0]
+
+        rows = [back(rows, i) for i in range(8)]
+        rights = [back(rights, i) for i in range(8)]
         for m in range(m0 + 1, 16):
             factors = [jnp.broadcast_to(left[m][:, j0 + i:j0 + i + 1], full) for i in range(8)]
             for side, vectors in ((left, rows), (right, rights)):

time: 60.1 us -> 59.8 us (level)
  no operation moved by 1% of the time
where the time goes in v7:
time: 59.8 us; the launch traced here: 59.6 us
  Pallas kernels  57.6 us (96%)
  local copies, waits for them, and re-layouts  1.35 us (2%)
  between operations  0.64 us (1%)
    pallas_call x1, Pallas kernels, panel(): pl.pallas_call(panel_kernel, out_shape=jax.ShapeDtypeStruct((2, 32, 128),...  57.6 us
    squeeze x1, local copies, waits for them, and re-layouts, local(): return (both[0], both[1])  1.35 us

profile of v7, /device:TPU:1, one launch (start us, length us, event | category | flops | bytes accessed | tf_op | source)
XLA Modules:
  0.0 59.6 jit_solution(12371437423530362878)
XLA Ops:
  0.6 57.6 %panel.1 = f32[2,32,128]{2,1,0:T(8,128)} custom-call(s32[1,32]{1,0:T(1,128)} %order_hbm.1, bf16[49,8,32]{2,1,0:T(8,128)(2,1)} %bitcast.8, bf16[32,8,49]{2,1,0:T(8,128)(2,1)} %g_hbm.1, f32[1,128]{1,0:T(1,128)} %bitcast.9), custom_call_target="tpu_custom_call" | custom-call | tf_op jit(solution)/shard_map/panel/pallas_call | solution.py:372
  58.3 1.3 %slice_bitcast_fusion = (f32[32,128]{1,0:T(8,128)}, f32[32,128]{1,0:T(8,128)}) fusion(f32[2,32,128]{2,1,0:T(8,128)} %panel.1), kind=kLoop, calls=%fused_computation | loop fusion | bytes 65536 | tf_op jit(solution)/shard_map/squeeze | solution.py:405

commit v8 on v6

--- a/solution.py
+++ b/solution.py
@@ -90,13 +90,15 @@
 
 
 def block(piv_ref, out_ref, ag, ax, bg, bx, gg, xx, yx):
-    for z2 in range(2):
-        for u in range(4):
-            chunk = (u * 2 + z2) * 2
-            split(z2, u, piv_ref[chunk], piv_ref[chunk + 1], bg, bx)
     dims = (((0,), (0,)), ((), ()))
-    gg[...] = lax.dot_general(ag[...], bg[...], dims, preferred_element_type=F32)
-    xx[...] = lax.dot_general(ax[...], bx[...], dims, preferred_element_type=F32)
+    for pair in range(2):
+        for u in (2 * pair, 2 * pair + 1):
+            for z2 in range(2):
+                chunk = (u * 2 + z2) * 2
+                split(z2, u, piv_ref[chunk], piv_ref[chunk + 1], bg, bx)
+        at = slice(None), pl.ds(pair * 256, 256)
+        gg[at] = lax.dot_general(ag[...], bg[at], dims, preferred_element_type=F32)
+        xx[at] = lax.dot_general(ax[...], bx[at], dims, preferred_element_type=F32)
     lanes = lax.broadcasted_iota(jnp.int32, (128, 128), 0)
     cols = lax.broadcasted_iota(jnp.int32, (128, 128), 1)
     piv0 = 16 * (yx % 2) + 2 * ((yx // 4) * 2 + (yx % 4) // 2)

time: 60.1 us -> 60.6 us (level)
  no operation moved by 1% of the time
where the time goes in v8:
time: 60.6 us; the launch traced here: 60.4 us
  Pallas kernels  58.5 us (97%)
  local copies, waits for them, and re-layouts  1.35 us (2%)
  between operations  0.64 us (1%)
    pallas_call x1, Pallas kernels, panel(): pl.pallas_call(panel_kernel, out_shape=jax.ShapeDtypeStruct((2, 32, 128),...  58.5 us
    squeeze x1, local copies, waits for them, and re-layouts, local(): return (both[0], both[1])  1.35 us

profile of v8, /device:TPU:1, one launch (start us, length us, event | category | flops | bytes accessed | tf_op | source)
XLA Modules:
  0.0 60.4 jit_solution(11805438297001489467)
XLA Ops:
  0.6 58.5 %panel.1 = f32[2,32,128]{2,1,0:T(8,128)} custom-call(s32[1,32]{1,0:T(1,128)} %order_hbm.1, bf16[49,8,32]{2,1,0:T(8,128)(2,1)} %bitcast.8, bf16[32,8,49]{2,1,0:T(8,128)(2,1)} %g_hbm.1, f32[1,128]{1,0:T(1,128)} %bitcast.9), custom_call_target="tpu_custom_call" | custom-call | tf_op jit(solution)/shard_map/panel/pallas_call | solution.py:366
  59.1 1.3 %slice_bitcast_fusion = (f32[32,128]{1,0:T(8,128)}, f32[32,128]{1,0:T(8,128)}) fusion(f32[2,32,128]{2,1,0:T(8,128)} %panel.1), kind=kLoop, calls=%fused_computation | loop fusion | bytes 65536 | tf_op jit(solution)/shard_map/squeeze | solution.py:399
